TPU v7x, 32 devices: a whole 2x2x4 slice. The times are simulated.
32 devices in a mesh: seq: 4 (over y, x), tensor: 8 (over z, core).
Axes of the slice: x: 2, y: 2, z: 4, core: 2. Of those that a mesh axis runs over, the one named last changes fastest.
Arguments:
- inputs: bfloat16 [768, 8192], P(('seq', 'tensor')), may hold values from -6 to 6
- grad_out: bfloat16 [768, 8192], P(('seq', 'tensor')), may hold values from -6 to 6
- up_blocks: bfloat16 [224, 8, 128, 128], P('tensor'), may hold values from -0.1875 to 0.1875
- up_index: int32 [224, 8], P('tensor'), may hold values from 0 to 63, as said below
- down_blocks: bfloat16 [224, 8, 128, 128], P('tensor'), may hold values from -0.1875 to 0.1875
- down_index: int32 [224, 8], P('tensor'), may hold values from 0 to 63, as said below
Outputs:
- grad_in: bfloat16 [768, 8192], P(('seq', 'tensor'))
- grad_up: bfloat16 [224, 8, 128, 128], P('tensor', None, 'seq')
- grad_down: bfloat16 [224, 8, 128, 128], P('tensor', None, 'seq')
Inputs may be any that keep to these rules, and one draw needn't show every extreme that they name: `up_index`: in every row the 8 block numbers are different, and every number from 0 to 63 appears in some row. `down_index`: in every row the 8 block numbers are different, and every number from 0 to 63 appears in some row.
All inputs are finite; a program needn't handle non-finite values.
Results may differ from a plain program's by a relative error of at most 0.012.
Values may be sent and summed in bfloat16 or wider, within the bound.
A program may use at most 128 MiB of HBM per device.

v0:
```python
import math

import jax
import jax.numpy as jnp
from jax import lax
from jax.sharding import PartitionSpec as P


def local(inputs, grad_out, up_blocks, up_index, down_blocks, down_index):
    tensor_count = lax.axis_size("tensor")
    seq_count = lax.axis_size("seq")
    rows_here, features = inputs.shape
    local_blocks, slots, block, _ = up_blocks.shape
    blocks_wide = features // block
    group_rows = rows_here * tensor_count
    factor = 1.0 / math.sqrt(group_rows * seq_count)
    flat_index = up_index.reshape(-1)
    in_rows = lax.all_gather(inputs, "tensor", axis=0, tiled=True)
    grad_rows = lax.all_gather(grad_out, "tensor", axis=0, tiled=True)
    piece_rows = in_rows.shape[0]
    picked = jnp.take(in_rows.reshape(piece_rows, blocks_wide, block), up_index, axis=1)
    picked_grad = jnp.take(grad_rows.reshape(piece_rows, blocks_wide, block), down_index, axis=1)
    preact = jnp.einsum("rjkc,jkch->rjh", picked, up_blocks, preferred_element_type=jnp.float32)
    hidden_grad = jnp.einsum(
        "rjko,jkho->rjh", picked_grad, down_blocks, preferred_element_type=jnp.float32
    )
    gating = jax.nn.sigmoid(preact)
    activated = (preact * gating).astype(jnp.bfloat16)
    preact_grad = (hidden_grad * gating * (1.0 + preact * (1.0 - gating))).astype(jnp.bfloat16)
    up_sum = jnp.einsum("rjkc,rjh->jkch", picked, preact_grad, preferred_element_type=jnp.float32)
    down_sum = jnp.einsum(
        "rjh,rjko->jkho", activated, picked_grad, preferred_element_type=jnp.float32
    )
    contrib = jnp.einsum(
        "rjh,jkch->rjkc", preact_grad, up_blocks, preferred_element_type=jnp.float32
    )
    contrib = contrib.reshape(piece_rows, local_blocks * slots, block)
    partial_value = (
        jnp.zeros((piece_rows, blocks_wide, block), jnp.float32).at[:, flat_index].add(contrib)
    )
    input_grad = partial_value
    up_sum, down_sum, input_grad = (up_sum, down_sum, input_grad)
    share = block // seq_count
    up_part = (
        (up_sum * factor).astype(jnp.bfloat16).reshape(local_blocks, slots, seq_count, share, block)
    )
    down_part = (
        (down_sum * factor)
        .astype(jnp.bfloat16)
        .reshape(local_blocks, slots, seq_count, share, block)
    )
    up_recv, down_recv = (
        lax.all_to_all(up_part, "seq", split_axis=2, concat_axis=2, tiled=True),
        lax.all_to_all(down_part, "seq", split_axis=2, concat_axis=2, tiled=True),
    )
    grad_up = jnp.sum(up_recv.astype(jnp.float32), axis=2).astype(jnp.bfloat16)
    grad_down = jnp.sum(down_recv.astype(jnp.float32), axis=2).astype(jnp.bfloat16)
    partial_rows = input_grad.reshape(group_rows, features).astype(jnp.bfloat16)
    pieces = partial_rows.reshape(tensor_count, rows_here, features)
    received = lax.all_to_all(pieces, "tensor", split_axis=0, concat_axis=0, tiled=True)
    grad_in = jnp.sum(received.astype(jnp.float32), axis=0).astype(jnp.bfloat16)
    return (grad_in, grad_up, grad_down)


def solution(mesh):
    return jax.shard_map(
        local,
        mesh=mesh,
        in_specs=(
            P(("seq", "tensor"), None),
            P(("seq", "tensor"), None),
            P("tensor", None, None, None),
            P("tensor", None),
            P("tensor", None, None, None),
            P("tensor", None),
        ),
        out_specs=(
            P(("seq", "tensor"), None),
            P("tensor", None, "seq", None),
            P("tensor", None, "seq", None),
        ),
        check_vma=False,
    )
```

profile of v0, /device:TPU:0, one launch (start us, length us, event | category | flops | bytes accessed | tf_op | source)
XLA Modules:
  0.0 400.7 jit_solution(1507287119658398462)
XLA Ops:
  7.2 0.0 all-gather.3.cloned.1.call-start
  7.2 0.7 all-gather.3.cloned.1.call-update
  7.9 0.0 all-gather.5.cloned.1.call-start
  7.9 0.7 all-gather.5.cloned.1.call-update
  8.6 0.7 compare_and_fusion
  9.3 0.1 copy.36
  9.5 0.7 compare_and_fusion.1
  10.1 0.1 copy.33
  10.3 0.7 compare_select_fusion
  10.9 0.1 copy.37
  11.0 0.1 reshape.99
  11.1 0.7 compare_select_fusion.1
  11.8 0.1 copy.34
  11.9 0.1 reshape.95
  12.0 38.6 %all-gather.3.cloned.1.call-done = bf16[192,8192]{1,0:T(8,128)(2,1)} async-done(((bf16[24,8192]{1,0:T(8,128)(2,1)}), bf16[192,8192]{1,0:T(8,128)(2,1)}) %all-gather.3.cloned.1.call-update) | async-done | bytes 3145744 | tf_op jit(solution)/shard_map/all_gather | solution.py:19
  50.7 2.8 copy_bitcast_fusion.1
  53.4 10.1 %gather_fusion = bf16[224,192,128]{2,1,0:T(8,128)(2,1)} fusion(bf16[192,64,128]{2,0,1:T(8,128)(2,1)S(1)} %copy_bitcast_fusion.1, s32[1024]{0:T(1024)S(1)} %pad_clamp_fusion.1), kind=kCustom, calls=%fused_computation.clone | custom fusion | bytes 22020992 | tf_op jit(solution)/shard_map/jit(_take)/gather | solution.py:22
  63.5 26.0 %all-gather.5.cloned.1.call-done = bf16[192,8192]{1,0:T(8,128)(2,1)} async-done(((bf16[24,8192]{1,0:T(8,128)(2,1)}), bf16[192,8192]{1,0:T(8,128)(2,1)}) %all-gather.5.cloned.1.call-update) | async-done | bytes 3145744 | tf_op jit(solution)/shard_map/all_gather | solution.py:18
  89.5 2.8 copy_bitcast_fusion
  92.3 10.2 %gather_fusion.1 = bf16[224,192,128]{2,1,0:T(8,128)(2,1)} fusion(bf16[192,64,128]{2,0,1:T(8,128)(2,1)S(1)} %copy_bitcast_fusion, s32[1024]{0:T(1024)S(1)} %pad_clamp_fusion), kind=kCustom, calls=%fused_computation.1.clone | custom fusion | bytes 22020992 | tf_op jit(solution)/shard_map/jit(_take)/gather | solution.py:21
  102.5 9.3 %fusion.2 = f32[28,192,128,1]{2,1,3,0:T(8,128)S(1)} fusion(bf16[28,8,128,128]{3,2,1,0:T(8,128)(2,1)} %param.10, bf16[28,8,192,128]{3,2,1,0:T(8,128)(2,1)} %bitcast.99, pred[28,8]{1,0:T(8,128)(4,1)S(1)} %copy.36), kind=kOutput, calls=%fused_computation.7 | convolution fusion | flops 1414791168 | bytes 21102816 | tf_op jit(solution)/shard_map/rjkc,jkch->rjh/dot_general | solution.py:23
  111.8 0.0 copy-start.1
  111.8 1.5 copy-done.1
  113.3 10.0 %fusion.16 = bf16[28,8,128,128]{2,3,1,0:T(8,128)(2,1)} fusion(bf16[28,8,192,128]{3,2,1,0:T(8,128)(2,1)} %bitcast.97, pred[28,8]{1,0:T(8,128)(4,1)S(1)} %copy.33, f32[28,192,128,1]{2,1,3,0:T(8,128)S(1)} %fusion.2), kind=kOutput, calls=%fused_computation.19 | convolution fusion | flops 1425571840 | bytes 21102816 | tf_op jit(solution)/shard_map/rjh,rjko->jkho/dot_general | solution.py:31
  123.3 10.4 %copy.42 = bf16[28,8,128,128]{3,2,1,0:T(8,128)(2,1)} copy(bf16[28,8,128,128]{2,3,1,0:T(8,128)(2,1)} %fusion.16) | data formatting | bytes 14680064 | tf_op jit(solution)/shard_map/convert_element_type | solution.py:49
  133.7 8.4 %copy.43 = bf16[28,8,4,32,128]{4,3,1,0,2:T(8,128)(2,1)} copy(bf16[28,8,4,32,128]{4,3,2,1,0:T(8,128)(2,1)} %bitcast.96) | data formatting | bytes 14680064 | tf_op jit(solution)/shard_map/reshape | solution.py:50
  142.1 5.5 %all-to-all-start.2 = ((bf16[28,8,4,32,128]{4,3,1,0,2:T(8,128)(2,1)}), bf16[28,8,4,32,128]{4,3,1,0,2:T(8,128)(2,1)}, u32[]{:S(2)}, u32[]{:S(2)}) async-start(bf16[28,8,4,32,128]{4,3,1,0,2:T(8,128)(2,1)} %copy.43), calls=%async_computation.2 | async-start | bytes 14680064 | tf_op jit(solution)/shard_map/all_to_all | solution.py:54
  147.6 10.3 %fusion.28 = bf16[192,28,128,1]{2,0,3,1:T(8,128)(2,1)S(1)} fusion(f32[28,192,128,1]{2,1,3,0:T(8,128)} %copy-done.1, bf16[28,8,128,128]{3,2,1,0:T(8,128)(2,1)} %param.12, bf16[28,8,192,128]{3,2,1,0:T(8,128)(2,1)} %bitcast.98, pred[28,8]{1,0:T(8,128)(4,1)S(1)} %copy.33), kind=kOutput, calls=%fused_computation.33 | convolution fusion | flops 1420984320 | bytes 22479072 | tf_op jit(solution)/shard_map/rjko,jkho->rjh/dot_general | solution.py:24
  157.9 7.7 %multiply_convert_fusion.1 = bf16[28,8,128,128]{3,2,1,0:T(8,128)(2,1)S(1)} fusion(bf16[192,28,128,1]{2,0,3,1:T(8,128)(2,1)S(1)} %fusion.28, bf16[28,8,192,128]{3,2,1,0:T(8,128)(2,1)} %bitcast.100, pred[28,8]{1,0:T(8,128)(4,1)S(1)} %copy.36), kind=kOutput, calls=%fused_computation.4 | convolution fusion | flops 1422131200 | bytes 19726560 | tf_op jit(solution)/shard_map/rjkc,rjh->jkch/dot_general | solution.py:30
  165.6 5.3 %copy.40 = bf16[28,8,4,32,128]{4,3,1,0,2:T(8,128)(2,1)} copy(bf16[28,8,4,32,128]{4,3,2,1,0:T(8,128)(2,1)S(1)} %bitcast.101) | data formatting | bytes 14680064 | tf_op jit(solution)/shard_map/reshape | solution.py:45
  170.9 0.0 copy-start
  170.9 58.4 %all-to-all-done.2 = bf16[28,8,4,32,128]{4,3,1,0,2:T(8,128)(2,1)} async-done(((bf16[28,8,4,32,128]{4,3,1,0,2:T(8,128)(2,1)}), bf16[28,8,4,32,128]{4,3,1,0,2:T(8,128)(2,1)}, u32[]{:S(2)}, u32[]{:S(2)}) %all-to-all-start.2) | async-done | bytes 7340064 | tf_op jit(solution)/shard_map/all_to_all | solution.py:54
  229.4 5.7 %all-to-all-start.1 = ((bf16[28,8,4,32,128]{4,3,1,0,2:T(8,128)(2,1)}), bf16[28,8,4,32,128]{4,3,1,0,2:T(8,128)(2,1)}, u32[]{:S(2)}, u32[]{:S(2)}) async-start(bf16[28,8,4,32,128]{4,3,1,0,2:T(8,128)(2,1)} %copy.40), calls=%async_computation.1 | async-start | bytes 14680064 | tf_op jit(solution)/shard_map/all_to_all | solution.py:53
  235.1 0.0 copy-done
  235.1 0.1 copy.32
  235.2 0.1 reshape.61
  235.3 13.4 %fusion.38 = f32[28,192,8,128]{3,1,2,0:T(8,128)} fusion(bf16[192,28,128,1]{2,0,3,1:T(8,128)(2,1)S(1)} %fusion.28, bf16[28,8,128,128]{3,2,1,0:T(8,128)(2,1)} %param.10), kind=kOutput, calls=%fused_computation.47 | convolution fusion | flops 1409286144 | bytes 30736384 | tf_op jit(solution)/shard_map/rjh,jkch->rjkc/dot_general | solution.py:34
  248.7 3.3 broadcast_in_dim.13
  252.0 56.7 %scatter_fusion = f32[192,64,128]{2,0,1:T(8,128)} fusion(f32[192,64,128]{2,0,1:T(8,128)} %broadcast_in_dim.13, s32[224]{0:T(256)S(1)} %bitcast.102, f32[224,192,128]{2,1,0:T(8,128)} %bitcast.95), kind=kCustom, calls=%fused_computation.2 | custom fusion | flops 5505024 | bytes 66061184 | tf_op jit(solution)/shard_map/scatter-add | solution.py:39
  308.8 3.3 convert_element_type.29
  312.1 2.0 copy.39
  314.1 3.3 convert_element_type.30
  317.5 0.0 all-to-all-done.1
  317.5 3.9 all-to-all-start
  321.4 6.2 %reduce_sum.38 = bf16[28,8,32,128]{3,2,1,0:T(8,128)(2,1)} reduce(bf16[28,8,4,32,128]{4,3,1,0,2:T(8,128)(2,1)} %all-to-all-done.2, bf16[]{:T(256)} %constant.11.clone.1), dimensions={2}, to_apply=%region_3.5 | reduce | flops 2752512 | bytes 9175042 | tf_op jit(solution)/shard_map/reduce_sum | solution.py:57
  327.6 6.2 %reduce_sum.37 = bf16[28,8,32,128]{3,2,1,0:T(8,128)(2,1)} reduce(bf16[28,8,4,32,128]{4,3,1,0,2:T(8,128)(2,1)} %all-to-all-done.1, bf16[]{:T(256)} %constant.11.clone.1), dimensions={2}, to_apply=%region_2.4 | reduce | flops 2752512 | bytes 9175042 | tf_op jit(solution)/shard_map/reduce_sum | solution.py:56
  333.9 58.7 %all-to-all-done = bf16[8,24,8192]{2,1,0:T(8,128)(2,1)S(1)} async-done(((bf16[8,24,8192]{2,1,0:T(8,128)(2,1)}), bf16[8,24,8192]{2,1,0:T(8,128)(2,1)S(1)}, u32[]{:S(2)}, u32[]{:S(2)}) %all-to-all-start) | async-done | bytes 3145760 | tf_op jit(solution)/shard_map/all_to_all | solution.py:60
  392.6 1.3 reduce_sum.36
  (3 shorter events, 0.0 us)
Async XLA Ops:
  7.2 43.5 %all-gather.3.cloned.1.call-start = ((), (), s32[]{:S(2)}) async-start(), calls=%async_computation.3 | async-start | bytes 3538944 | tf_op jit(solution)/shard_map/all_gather | solution.py:19
  7.9 81.6 %all-gather.5.cloned.1.call-start = ((), (), s32[]{:S(2)}) async-start(), calls=%async_computation.4 | async-start | bytes 3538944 | tf_op jit(solution)/shard_map/all_gather | solution.py:18
  111.8 1.5 copy-start.1
  142.1 87.3 %all-to-all-start.2 = ((bf16[28,8,4,32,128]{4,3,1,0,2:T(8,128)(2,1)}), bf16[28,8,4,32,128]{4,3,1,0,2:T(8,128)(2,1)}, u32[]{:S(2)}, u32[]{:S(2)}) async-start(bf16[28,8,4,32,128]{4,3,1,0,2:T(8,128)(2,1)} %copy.43), calls=%async_computation.2 | async-start | bytes 14680064 | tf_op jit(solution)/shard_map/all_to_all | solution.py:54
  170.9 64.1 %copy-start = (s32[28,8]{0,1:T(8,128)S(1)}, s32[28,8]{0,1:T(8,128)}, u32[]{:S(2)}) copy-start(s32[28,8]{0,1:T(8,128)} %param.11) | copy-start | bytes 2692
  229.4 88.1 %all-to-all-start.1 = ((bf16[28,8,4,32,128]{4,3,1,0,2:T(8,128)(2,1)}), bf16[28,8,4,32,128]{4,3,1,0,2:T(8,128)(2,1)}, u32[]{:S(2)}, u32[]{:S(2)}) async-start(bf16[28,8,4,32,128]{4,3,1,0,2:T(8,128)(2,1)} %copy.40), calls=%async_computation.1 | async-start | bytes 14680064 | tf_op jit(solution)/shard_map/all_to_all | solution.py:53
  317.5 75.1 %all-to-all-start = ((bf16[8,24,8192]{2,1,0:T(8,128)(2,1)}), bf16[8,24,8192]{2,1,0:T(8,128)(2,1)S(1)}, u32[]{:S(2)}, u32[]{:S(2)}) async-start(bf16[8,24,8192]{2,1,0:T(8,128)(2,1)} %convert_element_type.30), calls=%async_computation | async-start | bytes 6291456 | tf_op jit(solution)/shard_map/all_to_all | solution.py:60
Sparse Core Ops, SparseCore 0:
  9.6 40.9 all-gather.2
  52.3 37.1 all-gather.4
where the time goes:
time: 402 us; the launch traced here: 401 us
  waiting for transfers between devices  183 us (46%)
  other arithmetic  76.6 us (19%)
  local copies, waits for them, and re-layouts  60.8 us (15%)
  matrix products  50.8 us (13%)
  starting transfers between devices  15.1 us (4%)
  between operations  14.2 us (4%)
    all_to_all x1, waiting for transfers between devices, local(): lax.all_to_all(pieces, 'tensor', split_axis=0, concat_axis=0, tiled=True)  58.7 us
    all_to_all x1, waiting for transfers between devices, local(): lax.all_to_all(down_part, 'seq', split_axis=2, concat_axis=2, tiled=True)  58.4 us
    scatter-add x1, other arithmetic, local(): jnp.zeros((piece_rows, blocks_wide, block), jnp.float32).at[:, flat_index]  56.7 us
    all_gather x1, waiting for transfers between devices, local(): grad_rows = lax.all_gather(grad_out, 'tensor', axis=0, tiled=True)  38.6 us
    all_gather x1, waiting for transfers between devices, local(): in_rows = lax.all_gather(inputs, 'tensor', axis=0, tiled=True)  26 us
    dot_general x1, matrix products, local(): jnp.einsum('rjh,jkch->rjkc', preact_grad, up_blocks, preferred_element_ty...  13.4 us
    convert_element_type x1, local copies, waits for them, and re-layouts, local(): down_part = (down_sum * factor).astype(jnp.bfloat16).reshape(local_blocks...  10.4 us
    dot_general x1, matrix products, local(): jnp.einsum('rjko,jkho->rjh', picked_grad, down_blocks, preferred_element_...  10.3 us
  transfers between devices with their start and end apart: 5, of which 4 were waited for; matrix products, arithmetic and copies ran while one was open for 34% of the time, Pallas kernels for 0%

commit v1 on v0

--- a/solution.py
+++ b/solution.py
@@ -1,9 +1,349 @@
+import functools
 import math
 
 import jax
 import jax.numpy as jnp
 from jax import lax
+from jax.experimental import pallas as pl
+from jax.experimental.pallas import tpu as pltpu
 from jax.sharding import PartitionSpec as P
+
+MESH = pl.DeviceIdType.MESH
+MIB = 1024 * 1024
+
+
+def gather_kernel(
+    zs, in_ref, go_ref, out, loc, own_send, own_recv, recv, zsend, xysend, hsend, sib_send, sib_recv
+):
+    s, t = lax.axis_index("seq"), lax.axis_index("tensor")
+    z, c = t // 2, t % 2
+    x, y = s % 2, s // 2
+    xn, yn, dg = y * 2 + (1 - x), (1 - y) * 2 + x, (1 - y) * 2 + (1 - x)
+    sib = z * 2 + (1 - c)
+
+    barrier = pltpu.get_barrier_semaphore()
+    for dev in ((s, sib), (xn, t), (yn, t)):
+        pl.semaphore_signal(barrier, inc=1, device_id=dev, device_id_type=MESH)
+
+    @pl.when(z < zs - 1)
+    def _():
+        pl.semaphore_signal(barrier, inc=1, device_id=(s, t + 2), device_id_type=MESH)
+
+    @pl.when(z > 0)
+    def _():
+        pl.semaphore_signal(barrier, inc=1, device_id=(s, t - 2), device_id_type=MESH)
+
+    pl.semaphore_wait(barrier, 3 + jnp.minimum(z, 1) + jnp.minimum(zs - 1 - z, 1))
+
+    def copy(ref, send, recv_sem, dev):
+        return pltpu.make_async_remote_copy(
+            src_ref=ref, dst_ref=ref, send_sem=send, recv_sem=recv_sem, device_id=dev, device_id_type=MESH
+        )
+
+    def own_copy(a, ref):
+        return pltpu.make_async_remote_copy(
+            src_ref=ref,
+            dst_ref=out.at[a, s, z, c],
+            send_sem=own_send.at[a],
+            recv_sem=own_recv.at[a],
+            device_id=(s, sib),
+            device_id_type=MESH,
+        )
+
+    def unit(q, o):
+        return out.at[c, q, o]
+
+    def right(o):
+        return copy(unit(s, o), zsend.at[0, o], recv.at[s, o, 0], (s, t + 2))
+
+    def left(o):
+        return copy(unit(s, o), zsend.at[1, o], recv.at[s, o, 0], (s, t - 2))
+
+    def to_x(o):
+        return copy(unit(s, o), xysend.at[0, o], recv.at[s, o, 0], (xn, t))
+
+    def to_y(o):
+        return copy(unit(s, o), xysend.at[1, o], recv.at[s, o, 0], (yn, t))
+
+    def half_y(o):
+        return copy(out.at[c, xn, o, 0], hsend.at[0, o], recv.at[xn, o, 0], (yn, t))
+
+    def half_x(o):
+        return copy(out.at[c, yn, o, 1], hsend.at[1, o], recv.at[yn, o, 1], (xn, t))
+
+    def to_sib(q, o):
+        return copy(unit(q, o), sib_send.at[q, o], sib_recv.at[q, o], (s, sib))
+
+    def from_sib(q, o):
+        return copy(out.at[1 - c, q, o], sib_send.at[q, o], sib_recv.at[q, o], (s, sib))
+
+    def got(q, o):
+        copy(unit(q, o), xysend.at[0, o], recv.at[q, o, 0], (xn, t)).wait_recv()
+
+    def got_half(o, h):
+        copy(out.at[c, dg, o, h], hsend.at[h, o], recv.at[dg, o, h], (xn, t)).wait_recv()
+
+    def spread(o):
+        to_x(o).start()
+        to_y(o).start()
+
+    def from_xy(o):
+        got(xn, o)
+        half_y(o).start()
+        to_sib(xn, o).start()
+        got(yn, o)
+        half_x(o).start()
+        to_sib(yn, o).start()
+
+    def from_diagonal(o):
+        got_half(o, 0)
+        got_half(o, 1)
+        to_sib(dg, o).start()
+
+    def at_distance(d, act):
+        if d == 0:
+            act(z)
+            return
+        pl.when(z - d >= 0)(lambda: act(z - d))
+        pl.when(z + d < zs)(lambda: act(z + d))
+
+    locals_ = [
+        pltpu.make_async_copy(ref, out.at[a, s, z, c], loc.at[a]) for a, ref in enumerate((in_ref, go_ref))
+    ]
+    owns = [own_copy(a, ref) for a, ref in enumerate((in_ref, go_ref))]
+    for one in owns + locals_:
+        one.start()
+    for one in locals_:
+        one.wait()
+    for one in owns:
+        one.wait_recv()
+
+    pl.when(z < zs - 1)(lambda: right(z).start())
+    pl.when(z > 0)(lambda: left(z).start())
+    spread(z)
+    for d in range(1, zs):
+
+        @pl.when(z - d >= 0)
+        def _(d=d):
+            o = z - d
+            got(s, o)
+            pl.when(z < zs - 1)(lambda: right(o).start())
+            spread(o)
+            to_sib(s, o).start()
+
+        @pl.when(z + d < zs)
+        def _(d=d):
+            o = z + d
+            got(s, o)
+            pl.when(z > 0)(lambda: left(o).start())
+            spread(o)
+            to_sib(s, o).start()
+
+        at_distance(d - 1, from_xy)
+        if d >= 2:
+            at_distance(d - 2, from_diagonal)
+    at_distance(zs - 1, from_xy)
+    if zs >= 2:
+        at_distance(zs - 2, from_diagonal)
+    at_distance(zs - 1, from_diagonal)
+
+    for one in owns:
+        one.wait_send()
+    for o in range(zs):
+        pl.when((o <= z) & (z < zs - 1))(lambda o=o: right(o).wait_send())
+        pl.when((o >= z) & (z > 0))(lambda o=o: left(o).wait_send())
+        to_x(o).wait_send()
+        to_y(o).wait_send()
+        half_y(o).wait_send()
+        half_x(o).wait_send()
+        for q in (xn, yn, dg):
+            to_sib(q, o).wait_send()
+            from_sib(q, o).wait_recv()
+
+        @pl.when(z != o)
+        def _(o=o):
+            to_sib(s, o).wait_send()
+            from_sib(s, o).wait_recv()
+
+
+def gather_all(inputs, grad_out, seqs, zs):
+    rows, features = inputs.shape
+    dma = pltpu.SemaphoreType.DMA
+    return pl.pallas_call(
+        functools.partial(gather_kernel, zs),
+        out_shape=jax.ShapeDtypeStruct((2, seqs, zs, 2, rows, features), inputs.dtype),
+        in_specs=[pl.BlockSpec(memory_space=pl.ANY)] * 2,
+        out_specs=pl.BlockSpec(memory_space=pl.ANY),
+        scratch_shapes=[
+            dma((2,)),
+            dma((2,)),
+            dma((2,)),
+            dma((seqs, zs, 2)),
+            dma((2, zs)),
+            dma((2, zs)),
+            dma((2, zs)),
+            dma((seqs, zs)),
+            dma((seqs, zs)),
+        ],
+        compiler_params=pltpu.CompilerParams(collective_id=0, has_side_effects=True),
+        name="gather_all",
+    )(inputs, grad_out)
+
+
+def picked_blocks(ref, index, j, slots, width):
+    return jnp.concatenate(
+        [ref[:, pl.ds(pl.multiple_of(index[j, k] * width, width), width)] for k in range(slots)], axis=1
+    )
+
+
+def forward(xs, gs, up, down):
+    slots, width, _ = up.shape
+    preact = jnp.dot(xs, up.reshape(slots * width, width), preferred_element_type=jnp.float32)
+    down_wide = jnp.concatenate([down[k] for k in range(slots)], axis=1)
+    hidden_grad = lax.dot_general(
+        gs, down_wide, (((1,), (1,)), ((), ())), preferred_element_type=jnp.float32
+    )
+    gating = jax.nn.sigmoid(preact)
+    pg = (hidden_grad * gating * (1.0 + preact * (1.0 - gating))).astype(jnp.bfloat16)
+    return (preact * gating).astype(jnp.bfloat16), pg
+
+
+def input_kernel(ui, di, pos, x_ref, g_ref, up_ref, down_ref, out_ref, acc):
+    j = pl.program_id(0)
+    slots, width = up_ref.shape[1], up_ref.shape[2]
+
+    @pl.when(j == 0)
+    def _():
+        acc[...] = jnp.zeros_like(acc)
+
+    xs = picked_blocks(x_ref, ui, j, slots, width)
+    gs = picked_blocks(g_ref, di, j, slots, width)
+    up = up_ref[0]
+    _, pg = forward(xs, gs, up, down_ref[0])
+    terms = lax.dot_general(
+        pg, up.reshape(slots * width, width), (((1,), (1,)), ((), ())), preferred_element_type=jnp.float32
+    )
+    for k in range(slots):
+        where = pl.ds(pl.multiple_of(ui[j, k] * width, width), width)
+        acc[:, where] += terms[:, k * width : (k + 1) * width]
+
+    @pl.when(j == pl.num_programs(0) - 1)
+    def _():
+        out_ref[...] = acc[...].astype(out_ref.dtype)
+
+
+def input_part(up_index, down_index, pos, both, up_blocks, down_blocks, rows):
+    count, slots, width, _ = up_blocks.shape
+    features = both.shape[2]
+    weight = pl.BlockSpec((1, slots, width, width), lambda j, *_: (j, 0, 0, 0))
+    return pl.pallas_call(
+        input_kernel,
+        out_shape=jax.ShapeDtypeStruct((rows, features), both.dtype),
+        grid_spec=pltpu.PrefetchScalarGridSpec(
+            num_scalar_prefetch=3,
+            grid=(count,),
+            in_specs=[
+                pl.BlockSpec(
+                    (None, rows, features), lambda j, ui, di, pos: (0, pos[0], 0), pipeline_mode=pl.Buffered(1)
+                ),
+                pl.BlockSpec(
+                    (None, rows, features), lambda j, ui, di, pos: (1, pos[0], 0), pipeline_mode=pl.Buffered(1)
+                ),
+                weight,
+                weight,
+            ],
+            out_specs=pl.BlockSpec((rows, features), lambda j, *_: (0, 0), pipeline_mode=pl.Buffered(1)),
+            scratch_shapes=[pltpu.VMEM((rows, features), jnp.float32)],
+        ),
+        compiler_params=pltpu.CompilerParams(vmem_limit_bytes=40 * MIB),
+        cost_estimate=pl.CostEstimate(
+            flops=6 * rows * count * slots * width * width,
+            bytes_accessed=4 * count * slots * width * width + 6 * rows * features,
+            transcendentals=rows * count * width,
+        ),
+        name="input_part",
+    )(up_index, down_index, pos, both, both, up_blocks, down_blocks)
+
+
+def grads_kernel(factor, ui, di, pos, x_ref, g_ref, up_ref, down_ref, gup_ref, gdown_ref, xq, turned):
+    j = pl.program_id(0)
+    slots, width = up_ref.shape[1], up_ref.shape[2]
+    share = gup_ref.shape[2]
+    mine = pl.ds(pl.multiple_of(pos[0] * share, share), share)
+
+    @pl.when(j == 0)
+    def _():
+        def one(b, carry):
+            turned[...] = x_ref[:, pl.ds(pl.multiple_of(b * width, width), width)].T
+            xq[b] = turned[mine, :]
+            return carry
+
+        lax.fori_loop(0, xq.shape[0], one, 0)
+
+    xs = picked_blocks(x_ref, ui, j, slots, width)
+    gs = picked_blocks(g_ref, di, j, slots, width)
+    activated, pg = forward(xs, gs, up_ref[0], down_ref[0])
+    quarter = jnp.concatenate([xq[ui[j, k]] for k in range(slots)], axis=0)
+    gup = jnp.dot(quarter, pg, preferred_element_type=jnp.float32) * factor
+    gup_ref[0] = gup.astype(gup_ref.dtype).reshape(slots, share, width)
+    turned[...] = activated.T
+    gdown = jnp.dot(turned[mine, :], gs, preferred_element_type=jnp.float32) * factor
+    for k in range(slots):
+        gdown_ref[0, k] = gdown[:, k * width : (k + 1) * width].astype(gdown_ref.dtype)
+
+
+def block_grads(up_index, down_index, pos, both, up_blocks, down_blocks, share, factor):
+    count, slots, width, _ = up_blocks.shape
+    _, tokens, features = both.shape
+    weight = pl.BlockSpec((1, slots, width, width), lambda j, *_: (j, 0, 0, 0))
+    result = pl.BlockSpec((1, slots, share, width), lambda j, *_: (j, 0, 0, 0))
+    shape = jax.ShapeDtypeStruct((count, slots, share, width), both.dtype)
+    return pl.pallas_call(
+        functools.partial(grads_kernel, factor),
+        out_shape=[shape, shape],
+        grid_spec=pltpu.PrefetchScalarGridSpec(
+            num_scalar_prefetch=3,
+            grid=(count,),
+            in_specs=[
+                pl.BlockSpec((None, tokens, features), lambda j, *_: (0, 0, 0), pipeline_mode=pl.Buffered(1)),
+                pl.BlockSpec((None, tokens, features), lambda j, *_: (1, 0, 0), pipeline_mode=pl.Buffered(1)),
+                weight,
+                weight,
+            ],
+            out_specs=[result, result],
+            scratch_shapes=[
+                pltpu.VMEM((features // width, share, tokens), both.dtype),
+                pltpu.VMEM((width, tokens), both.dtype),
+            ],
+        ),
+        compiler_params=pltpu.CompilerParams(vmem_limit_bytes=56 * MIB),
+        cost_estimate=pl.CostEstimate(
+            flops=6 * tokens * count * slots * width * width,
+            bytes_accessed=6 * count * slots * width * width + 4 * tokens * features,
+            transcendentals=tokens * count * width,
+        ),
+        name="block_grads",
+    )(up_index, down_index, pos, both, both, up_blocks, down_blocks)
+
+
+def local_all_tokens(inputs, grad_out, up_blocks, up_index, down_blocks, down_index):
+    tensor_count = lax.axis_size("tensor")
+    seq_count = lax.axis_size("seq")
+    rows_here, features = inputs.shape
+    block = up_blocks.shape[2]
+    group_rows = rows_here * tensor_count
+    factor = 1.0 / math.sqrt(group_rows * seq_count)
+    both = gather_all(inputs, grad_out, seq_count, tensor_count // 2)
+    both = both.reshape(2, group_rows * seq_count, features)
+    pos = lax.axis_index("seq").astype(jnp.int32).reshape(1)
+    part = input_part(up_index, down_index, pos, both, up_blocks, down_blocks, group_rows)
+    pieces = part.reshape(tensor_count, rows_here, features)
+    received = lax.all_to_all(pieces, "tensor", split_axis=0, concat_axis=0, tiled=True)
+    grad_up, grad_down = block_grads(
+        up_index, down_index, pos, both, up_blocks, down_blocks, block // seq_count, factor
+    )
+    grad_in = jnp.sum(received.astype(jnp.float32), axis=0).astype(jnp.bfloat16)
+    return (grad_in, grad_up, grad_down)
 
 
 def local(inputs, grad_out, up_blocks, up_index, down_blocks, down_index):
@@ -61,10 +401,10 @@
     grad_in = jnp.sum(received.astype(jnp.float32), axis=0).astype(jnp.bfloat16)
     return (grad_in, grad_up, grad_down)
 
-
 def solution(mesh):
+    gathers = mesh.shape["seq"] == 4 and mesh.shape["tensor"] % 2 == 0
     return jax.shard_map(
-        local,
+        local_all_tokens if gathers else local,
         mesh=mesh,
         in_specs=(
             P(("seq", "tensor"), None),

time: 402 us -> 250 us (0.62)
  Pallas kernels: 0 us -> 225 us
  waiting for transfers between devices: 183 us -> 13.2 us
  other arithmetic: 76.6 us -> 1.28 us
  local copies, waits for them, and re-layouts: 60.8 us -> 4.64 us
  matrix products: 50.8 us -> 0 us
  between operations: 14.2 us -> 0.67 us
  starting transfers between devices: 15.1 us -> 3.78 us
    pallas_call x0 -> x3, Pallas kernels: none -> 225 us  [the longest x1 136 us: gather_all(): pl.pallas_call(functools.partial(gather_kernel, zs), out_shape=jax.ShapeD...]
    all_to_all x3 -> x1, waiting for transfers between devices: 117 us -> 13.2 us  [local_all_tokens(): lax.all_to_all(pieces, 'tensor', split_axis=0, concat_axis=0, tiled=True)]
    all_gather x2 -> x0, waiting for transfers between devices: 64.6 us -> none  [the longest x1 38.6 us: local(): grad_rows = lax.all_gather(grad_out, 'tensor', axis=0, tiled=True)]
    scatter-add x1 -> x0, other arithmetic: 56.7 us -> none  [local(): jnp.zeros((piece_rows, blocks_wide, block), jnp.float32).at[:, flat_index]]
    dot_general x5 -> x0, matrix products: 50.8 us -> none  [the longest x1 13.4 us: local(): jnp.einsum('rjh,jkch->rjkc', preact_grad, up_blocks, preferred_element_ty...]
    gather x2 -> x0, local copies, waits for them, and re-layouts: 20.3 us -> none  [the longest x1 10.2 us: local(): jnp.take(in_rows.reshape(piece_rows, blocks_wide, block), up_index, axis=1)]
    reshape x5 -> x0, local copies, waits for them, and re-layouts: 19.3 us -> none  [the longest x1 8.38 us: local(): down_part = (down_sum * factor).astype(jnp.bfloat16).reshape(local_blocks...]
    convert_element_type x3 -> x0, local copies, waits for them, and re-layouts: 15.8 us -> none  [the longest x1 10.4 us: local(): down_part = (down_sum * factor).astype(jnp.bfloat16).reshape(local_blocks...]
  transfers between devices with their start and end apart: 5 -> 1, of which waited for: 4 -> 1; matrix products, arithmetic and copies ran while one was open for 34% -> 0% of each run, Pallas kernels for 0% -> 23%
where the time goes in v1:
time: 250 us; the launch traced here: 249 us
  Pallas kernels  225 us (90%)
  waiting for transfers between devices  13.2 us (5%)
  local copies, waits for them, and re-layouts  4.64 us (2%)
  starting transfers between devices  3.78 us (2%)
    pallas_call x1, Pallas kernels, gather_all(): pl.pallas_call(functools.partial(gather_kernel, zs), out_shape=jax.ShapeD...  136 us
    pallas_call x1, Pallas kernels, block_grads(): pl.pallas_call(functools.partial(grads_kernel, factor), out_shape=[shape,...  58.3 us
    pallas_call x1, Pallas kernels, input_part(): pl.pallas_call(input_kernel, out_shape=jax.ShapeDtypeStruct((rows, featur...  30.8 us
    all_to_all x1, waiting for transfers between devices, local_all_tokens(): lax.all_to_all(pieces, 'tensor', split_axis=0, concat_axis=0, tiled=True)  13.2 us
  transfers between devices with their start and end apart: 1, of which 1 were waited for; matrix products, arithmetic and copies ran while one was open for 0% of the time, Pallas kernels for 23%

profile of v1, /device:TPU:0, one launch (start us, length us, event | category | flops | bytes accessed | tf_op | source)
XLA Modules:
  0.0 249.0 jit_solution(10087495806714716646)
XLA Ops:
  0.6 0.8 copy.9.ui
  1.4 0.0 copy-start.1
  1.4 0.8 copy.10.di
  2.2 0.0 copy-start.2
  2.2 136.2 %gather_all.1 = bf16[2,4,4,2,24,8192]{5,4,3,2,1,0:T(8,128)(2,1)} custom-call(bf16[24,8192]{1,0:T(8,128)(2,1)} %in_ref.1, bf16[24,8192]{1,0:T(8,128)(2,1)} %go_ref.1), custom_call_target="tpu_custom_call" | custom-call | tf_op jit(solution)/shard_map/gather_all/pallas_call | solution.py:172
  138.4 0.0 copy-done.1
  138.4 0.0 copy-done.2
  138.5 0.0 copy-start
  138.5 3.1 %copy-done = bf16[28,8,128,128]{3,2,1,0:T(8,128)(2,1)S(1)} copy-done((bf16[28,8,128,128]{3,2,1,0:T(8,128)(2,1)S(1)}, bf16[28,8,128,128]{3,2,1,0:T(8,128)(2,1)}, u32[]{:S(2)}) %copy-start) | copy-done | bytes 7340056
  141.5 30.8 %input_part.1 = bf16[192,8192]{1,0:T(8,128)(2,1)} custom-call(s32[28,8]{1,0:T(8,128)S(1)} %copy.9.ui, s32[28,8]{1,0:T(8,128)S(1)} %copy.10.di, s32[1]{0:T(128)} %bitcast.pos, bf16[2,768,8192]{2,1,0:T(8,128)(2,1)} %bitcast.3, bf16[2,768,8192]{2,1,0:T(8,128)(2,1)} %bitcast.4, bf16[28,8,128,128]{3,2,1,0:T(8,128)(2,1)S(1)} %copy-done, ...), custom_call_target="tpu_custom_call" | custom-call | flops 4227858432 | bytes 24117248 | tf_op jit(solution)/shard_map/input_part/pallas_call | solution.py:239
  172.4 3.8 %all-to-all-start = ((bf16[8,24,8192]{2,1,0:T(8,128)(2,1)}), bf16[8,24,8192]{2,1,0:T(8,128)(2,1)S(1)}, u32[]{:S(2)}, u32[]{:S(2)}) async-start(bf16[8,24,8192]{2,1,0:T(8,128)(2,1)} %bitcast.2), calls=%async_computation | async-start | bytes 6291456 | tf_op jit(solution)/shard_map/all_to_all | solution.py:341
  176.2 58.3 %block_grads.1 = (bf16[28,8,32,128]{3,2,1,0:T(8,128)(2,1)}, bf16[28,8,32,128]{3,2,1,0:T(8,128)(2,1)}) custom-call(s32[28,8]{1,0:T(8,128)} %copy-done.1, s32[28,8]{1,0:T(8,128)} %copy-done.2, s32[1]{0:T(128)} %bitcast.pos, bf16[2,768,8192]{2,1,0:T(8,128)(2,1)} %bitcast.5, bf16[2,768,8192]{2,1,0:T(8,128)(2,1)} %bitcast.6, bf16[28,8,128,128]{3,2,1,0:T(8,128)(2,1)} %up_ref.3, ...), custom_call_target="tpu_custom_call" | custom-call | flops 16911433728 | bytes 47185920 | tf_op jit(solution)/shard_map/block_grads/pallas_call | solution.py:301
  234.5 13.2 %all-to-all-done = bf16[8,24,8192]{2,1,0:T(8,128)(2,1)S(1)} async-done(((bf16[8,24,8192]{2,1,0:T(8,128)(2,1)}), bf16[8,24,8192]{2,1,0:T(8,128)(2,1)S(1)}, u32[]{:S(2)}, u32[]{:S(2)}) %all-to-all-start) | async-done | bytes 3145760 | tf_op jit(solution)/shard_map/all_to_all | solution.py:341
  247.7 1.3 reduce_sum.12
Async XLA Ops:
  1.4 137.0 %copy-start.1 = (s32[28,8]{1,0:T(8,128)}, s32[28,8]{1,0:T(8,128)S(1)}, u32[]{:S(2)}) copy-start(s32[28,8]{1,0:T(8,128)S(1)} %copy.9.ui) | copy-start | bytes 2692
  2.2 136.3 %copy-start.2 = (s32[28,8]{1,0:T(8,128)}, s32[28,8]{1,0:T(8,128)S(1)}, u32[]{:S(2)}) copy-start(s32[28,8]{1,0:T(8,128)S(1)} %copy.10.di) | copy-start | bytes 2692
  138.5 3.1 %copy-start = (bf16[28,8,128,128]{3,2,1,0:T(8,128)(2,1)S(1)}, bf16[28,8,128,128]{3,2,1,0:T(8,128)(2,1)}, u32[]{:S(2)}) copy-start(bf16[28,8,128,128]{3,2,1,0:T(8,128)(2,1)} %up_ref.3) | copy-start | bytes 22020100
  172.4 75.3 %all-to-all-start = ((bf16[8,24,8192]{2,1,0:T(8,128)(2,1)}), bf16[8,24,8192]{2,1,0:T(8,128)(2,1)S(1)}, u32[]{:S(2)}, u32[]{:S(2)}) async-start(bf16[8,24,8192]{2,1,0:T(8,128)(2,1)} %bitcast.2), calls=%async_computation | async-start | bytes 6291456 | tf_op jit(solution)/shard_map/all_to_all | solution.py:341

commit v2 on v1

--- a/solution.py
+++ b/solution.py
@@ -216,16 +216,26 @@
     def _():
         acc[...] = jnp.zeros_like(acc)
 
-    xs = picked_blocks(x_ref, ui, j, slots, width)
-    gs = picked_blocks(g_ref, di, j, slots, width)
-    up = up_ref[0]
-    _, pg = forward(xs, gs, up, down_ref[0])
-    terms = lax.dot_general(
-        pg, up.reshape(slots * width, width), (((1,), (1,)), ((), ())), preferred_element_type=jnp.float32
-    )
-    for k in range(slots):
-        where = pl.ds(pl.multiple_of(ui[j, k] * width, width), width)
-        acc[:, where] += terms[:, k * width : (k + 1) * width]
+    together = up_ref.shape[0]
+    terms = []
+    for u in range(together):
+        row = j * together + u
+        xs = picked_blocks(x_ref, ui, row, slots, width)
+        gs = picked_blocks(g_ref, di, row, slots, width)
+        up = up_ref[u]
+        _, pg = forward(xs, gs, up, down_ref[u])
+        terms.append(
+            lax.dot_general(
+                pg,
+                up.reshape(slots * width, width),
+                (((1,), (1,)), ((), ())),
+                preferred_element_type=jnp.float32,
+            )
+        )
+    for u in range(together):
+        for k in range(slots):
+            where = pl.ds(pl.multiple_of(ui[j * together + u, k] * width, width), width)
+            acc[:, where] += terms[u][:, k * width : (k + 1) * width]
 
     @pl.when(j == pl.num_programs(0) - 1)
     def _():
@@ -235,13 +245,14 @@
 def input_part(up_index, down_index, pos, both, up_blocks, down_blocks, rows):
     count, slots, width, _ = up_blocks.shape
     features = both.shape[2]
-    weight = pl.BlockSpec((1, slots, width, width), lambda j, *_: (j, 0, 0, 0))
+    together = math.gcd(count, 4)
+    weight = pl.BlockSpec((together, slots, width, width), lambda j, *_: (j, 0, 0, 0))
     return pl.pallas_call(
         input_kernel,
         out_shape=jax.ShapeDtypeStruct((rows, features), both.dtype),
         grid_spec=pltpu.PrefetchScalarGridSpec(
             num_scalar_prefetch=3,
-            grid=(count,),
+            grid=(count // together,),
             in_specs=[
                 pl.BlockSpec(
                     (None, rows, features), lambda j, ui, di, pos: (0, pos[0], 0), pipeline_mode=pl.Buffered(1)
@@ -274,36 +285,42 @@
     @pl.when(j == 0)
     def _():
         def one(b, carry):
-            turned[...] = x_ref[:, pl.ds(pl.multiple_of(b * width, width), width)].T
-            xq[b] = turned[mine, :]
+            for u in range(turned.shape[0]):
+                block = b * turned.shape[0] + u
+                turned[u] = x_ref[:, pl.ds(pl.multiple_of(block * width, width), width)].T
+                xq[block] = turned[u, mine, :]
             return carry
 
-        lax.fori_loop(0, xq.shape[0], one, 0)
-
-    xs = picked_blocks(x_ref, ui, j, slots, width)
-    gs = picked_blocks(g_ref, di, j, slots, width)
-    activated, pg = forward(xs, gs, up_ref[0], down_ref[0])
-    quarter = jnp.concatenate([xq[ui[j, k]] for k in range(slots)], axis=0)
-    gup = jnp.dot(quarter, pg, preferred_element_type=jnp.float32) * factor
-    gup_ref[0] = gup.astype(gup_ref.dtype).reshape(slots, share, width)
-    turned[...] = activated.T
-    gdown = jnp.dot(turned[mine, :], gs, preferred_element_type=jnp.float32) * factor
-    for k in range(slots):
-        gdown_ref[0, k] = gdown[:, k * width : (k + 1) * width].astype(gdown_ref.dtype)
+        lax.fori_loop(0, xq.shape[0] // turned.shape[0], one, 0)
+
+    together = up_ref.shape[0]
+    for u in range(together):
+        row = j * together + u
+        xs = picked_blocks(x_ref, ui, row, slots, width)
+        gs = picked_blocks(g_ref, di, row, slots, width)
+        activated, pg = forward(xs, gs, up_ref[u], down_ref[u])
+        quarter = jnp.concatenate([xq[ui[row, k]] for k in range(slots)], axis=0)
+        gup = jnp.dot(quarter, pg, preferred_element_type=jnp.float32) * factor
+        gup_ref[u] = gup.astype(gup_ref.dtype).reshape(slots, share, width)
+        turned[u] = activated.T
+        gdown = jnp.dot(turned[u, mine, :], gs, preferred_element_type=jnp.float32) * factor
+        for k in range(slots):
+            gdown_ref[u, k] = gdown[:, k * width : (k + 1) * width].astype(gdown_ref.dtype)
 
 
 def block_grads(up_index, down_index, pos, both, up_blocks, down_blocks, share, factor):
     count, slots, width, _ = up_blocks.shape
     _, tokens, features = both.shape
-    weight = pl.BlockSpec((1, slots, width, width), lambda j, *_: (j, 0, 0, 0))
-    result = pl.BlockSpec((1, slots, share, width), lambda j, *_: (j, 0, 0, 0))
+    together = math.gcd(count, 2)
+    weight = pl.BlockSpec((together, slots, width, width), lambda j, *_: (j, 0, 0, 0))
+    result = pl.BlockSpec((together, slots, share, width), lambda j, *_: (j, 0, 0, 0))
     shape = jax.ShapeDtypeStruct((count, slots, share, width), both.dtype)
     return pl.pallas_call(
         functools.partial(grads_kernel, factor),
         out_shape=[shape, shape],
         grid_spec=pltpu.PrefetchScalarGridSpec(
             num_scalar_prefetch=3,
-            grid=(count,),
+            grid=(count // together,),
             in_specs=[
                 pl.BlockSpec((None, tokens, features), lambda j, *_: (0, 0, 0), pipeline_mode=pl.Buffered(1)),
                 pl.BlockSpec((None, tokens, features), lambda j, *_: (1, 0, 0), pipeline_mode=pl.Buffered(1)),
@@ -313,7 +330,7 @@
             out_specs=[result, result],
             scratch_shapes=[
                 pltpu.VMEM((features // width, share, tokens), both.dtype),
-                pltpu.VMEM((width, tokens), both.dtype),
+                pltpu.VMEM((together, width, tokens), both.dtype),
             ],
         ),
         compiler_params=pltpu.CompilerParams(vmem_limit_bytes=56 * MIB),

time: 250 us -> 241 us (0.964)
  Pallas kernels: 225 us -> 211 us
  waiting for transfers between devices: 13.2 us -> 19.1 us
    pallas_call x1, Pallas kernels: 30.8 us -> 22.2 us  [input_part(): pl.pallas_call(input_kernel, out_shape=jax.ShapeDtypeStruct((rows, featur...]
    all_to_all x1, waiting for transfers between devices: 13.2 us -> 19.1 us  [local_all_tokens(): lax.all_to_all(pieces, 'tensor', split_axis=0, concat_axis=0, tiled=True)]
    pallas_call x1, Pallas kernels: 58.3 us -> 52.4 us  [block_grads(): pl.pallas_call(functools.partial(grads_kernel, factor), out_shape=[shape,...]
  transfers between devices with their start and end apart: 1 -> 1, of which waited for: 1 -> 1; matrix products, arithmetic and copies ran while one was open for 0% -> 0% of each run, Pallas kernels for 23% -> 22%
where the time goes in v2:
time: 241 us; the launch traced here: 240 us
  Pallas kernels  211 us (88%)
  waiting for transfers between devices  19.1 us (8%)
  local copies, waits for them, and re-layouts  4.64 us (2%)
  starting transfers between devices  3.78 us (2%)
    pallas_call x1, Pallas kernels, gather_all(): pl.pallas_call(functools.partial(gather_kernel, zs), out_shape=jax.ShapeD...  136 us
    pallas_call x1, Pallas kernels, block_grads(): pl.pallas_call(functools.partial(grads_kernel, factor), out_shape=[shape,...  52.4 us
    pallas_call x1, Pallas kernels, input_part(): pl.pallas_call(input_kernel, out_shape=jax.ShapeDtypeStruct((rows, featur...  22.2 us
    all_to_all x1, waiting for transfers between devices, local_all_tokens(): lax.all_to_all(pieces, 'tensor', split_axis=0, concat_axis=0, tiled=True)  19.1 us
  transfers between devices with their start and end apart: 1, of which 1 were waited for; matrix products, arithmetic and copies ran while one was open for 0% of the time, Pallas kernels for 22%

profile of v2, /device:TPU:0, one launch (start us, length us, event | category | flops | bytes accessed | tf_op | source)
XLA Modules:
  0.0 240.4 jit_solution(9221679256798534132)
XLA Ops:
  0.6 0.8 copy.9.ui
  1.4 0.0 copy-start.1
  1.4 0.8 copy.10.di
  2.2 0.0 copy-start.2
  2.2 136.2 %gather_all.1 = bf16[2,4,4,2,24,8192]{5,4,3,2,1,0:T(8,128)(2,1)} custom-call(bf16[24,8192]{1,0:T(8,128)(2,1)} %in_ref.1, bf16[24,8192]{1,0:T(8,128)(2,1)} %go_ref.1), custom_call_target="tpu_custom_call" | custom-call | tf_op jit(solution)/shard_map/gather_all/pallas_call | solution.py:172
  138.4 0.0 copy-done.1
  138.4 0.0 copy-done.2
  138.5 0.0 copy-start
  138.5 3.1 %copy-done = bf16[28,8,128,128]{3,2,1,0:T(8,128)(2,1)S(1)} copy-done((bf16[28,8,128,128]{3,2,1,0:T(8,128)(2,1)S(1)}, bf16[28,8,128,128]{3,2,1,0:T(8,128)(2,1)}, u32[]{:S(2)}) %copy-start) | copy-done | bytes 7340056
  141.5 22.2 %input_part.1 = bf16[192,8192]{1,0:T(8,128)(2,1)} custom-call(s32[28,8]{1,0:T(8,128)S(1)} %copy.9.ui, s32[28,8]{1,0:T(8,128)S(1)} %copy.10.di, s32[1]{0:T(128)} %bitcast.pos, bf16[2,768,8192]{2,1,0:T(8,128)(2,1)} %bitcast.3, bf16[2,768,8192]{2,1,0:T(8,128)(2,1)} %bitcast.4, bf16[28,8,128,128]{3,2,1,0:T(8,128)(2,1)S(1)} %copy-done, ...), custom_call_target="tpu_custom_call" | custom-call | flops 4227858432 | bytes 24117248 | tf_op jit(solution)/shard_map/input_part/pallas_call | solution.py:250
  163.8 3.8 %all-to-all-start = ((bf16[8,24,8192]{2,1,0:T(8,128)(2,1)}), bf16[8,24,8192]{2,1,0:T(8,128)(2,1)S(1)}, u32[]{:S(2)}, u32[]{:S(2)}) async-start(bf16[8,24,8192]{2,1,0:T(8,128)(2,1)} %bitcast.2), calls=%async_computation | async-start | bytes 6291456 | tf_op jit(solution)/shard_map/all_to_all | solution.py:358
  167.5 52.4 %block_grads.1 = (bf16[28,8,32,128]{3,2,1,0:T(8,128)(2,1)}, bf16[28,8,32,128]{3,2,1,0:T(8,128)(2,1)}) custom-call(s32[28,8]{1,0:T(8,128)} %copy-done.1, s32[28,8]{1,0:T(8,128)} %copy-done.2, s32[1]{0:T(128)} %bitcast.pos, bf16[2,768,8192]{2,1,0:T(8,128)(2,1)} %bitcast.5, bf16[2,768,8192]{2,1,0:T(8,128)(2,1)} %bitcast.6, bf16[28,8,128,128]{3,2,1,0:T(8,128)(2,1)} %up_ref.3, ...), custom_call_target="tpu_custom_call" | custom-call | flops 16911433728 | bytes 47185920 | tf_op jit(solution)/shard_map/block_grads/pallas_call | solution.py:318
  220.0 19.1 %all-to-all-done = bf16[8,24,8192]{2,1,0:T(8,128)(2,1)S(1)} async-done(((bf16[8,24,8192]{2,1,0:T(8,128)(2,1)}), bf16[8,24,8192]{2,1,0:T(8,128)(2,1)S(1)}, u32[]{:S(2)}, u32[]{:S(2)}) %all-to-all-start) | async-done | bytes 3145760 | tf_op jit(solution)/shard_map/all_to_all | solution.py:358
  239.1 1.3 reduce_sum.12
Async XLA Ops:
  1.4 137.0 %copy-start.1 = (s32[28,8]{1,0:T(8,128)}, s32[28,8]{1,0:T(8,128)S(1)}, u32[]{:S(2)}) copy-start(s32[28,8]{1,0:T(8,128)S(1)} %copy.9.ui) | copy-start | bytes 2692
  2.2 136.3 %copy-start.2 = (s32[28,8]{1,0:T(8,128)}, s32[28,8]{1,0:T(8,128)S(1)}, u32[]{:S(2)}) copy-start(s32[28,8]{1,0:T(8,128)S(1)} %copy.10.di) | copy-start | bytes 2692
  138.5 3.1 %copy-start = (bf16[28,8,128,128]{3,2,1,0:T(8,128)(2,1)S(1)}, bf16[28,8,128,128]{3,2,1,0:T(8,128)(2,1)}, u32[]{:S(2)}) copy-start(bf16[28,8,128,128]{3,2,1,0:T(8,128)(2,1)} %up_ref.3) | copy-start | bytes 22020100
  163.8 75.3 %all-to-all-start = ((bf16[8,24,8192]{2,1,0:T(8,128)(2,1)}), bf16[8,24,8192]{2,1,0:T(8,128)(2,1)S(1)}, u32[]{:S(2)}, u32[]{:S(2)}) async-start(bf16[8,24,8192]{2,1,0:T(8,128)(2,1)} %bitcast.2), calls=%async_computation | async-start | bytes 6291456 | tf_op jit(solution)/shard_map/all_to_all | solution.py:358

commit v3 on v0

--- a/solution.py
+++ b/solution.py
@@ -1,9 +1,478 @@
+import functools
 import math
 
 import jax
 import jax.numpy as jnp
 from jax import lax
+from jax.experimental import pallas as pl
+from jax.experimental.pallas import tpu as pltpu
 from jax.sharding import PartitionSpec as P
+
+MESH = pl.DeviceIdType.MESH
+MIB = 1024 * 1024
+
+
+def place():
+    s, t = lax.axis_index("seq"), lax.axis_index("tensor")
+    z, c = t // 2, t % 2
+    x, y = s % 2, s // 2
+    xn, yn = y * 2 + (1 - x), (1 - y) * 2 + x
+    return s, t, z, c, (xn, t), (yn, t), (s, z * 2 + (1 - c))
+
+
+def remote(src, dst, send, recv, dev):
+    return pltpu.make_async_remote_copy(
+        src_ref=src, dst_ref=dst, send_sem=send, recv_sem=recv, device_id=dev, device_id_type=MESH
+    )
+
+
+def gather_kernel(
+    zs, in_ref, go_ref, out, loc, own_send, own_recv, zrecv, zsend, recv, send, sib_send, sib_recv
+):
+    s, t, z, c, xdev, ydev, sib = place()
+    r = z % 2
+    mate = z + 1 - 2 * r
+
+    barrier = pltpu.get_barrier_semaphore()
+    for dev in (sib, xdev, ydev):
+        pl.semaphore_signal(barrier, inc=1, device_id=dev, device_id_type=MESH)
+
+    @pl.when(z < zs - 1)
+    def _():
+        pl.semaphore_signal(barrier, inc=1, device_id=(s, t + 2), device_id_type=MESH)
+
+    @pl.when(z > 0)
+    def _():
+        pl.semaphore_signal(barrier, inc=1, device_id=(s, t - 2), device_id_type=MESH)
+
+    pl.semaphore_wait(barrier, 3 + jnp.minimum(z, 1) + jnp.minimum(zs - 1 - z, 1))
+
+    def unit(i):
+        return out.at[c, i]
+
+    def right(o):
+        return remote(unit(o), unit(o), zsend.at[0, o], zrecv.at[o], (s, t + 2))
+
+    def left(o):
+        return remote(unit(o), unit(o), zsend.at[1, o], zrecv.at[o], (s, t - 2))
+
+    def to_x(o, i):
+        return remote(unit(o), unit(zs + i), send.at[0, i], recv.at[0, i], xdev)
+
+    def to_y(o, i):
+        return remote(unit(o), unit(zs + 2 + i), send.at[1, i], recv.at[1, i], ydev)
+
+    def onward_y():
+        return remote(unit(zs), unit(zs + 4), send.at[2, 0], recv.at[2, 0], ydev)
+
+    def onward_x():
+        return remote(unit(zs + 3), unit(zs + 5), send.at[2, 1], recv.at[2, 1], xdev)
+
+    def to_sib(i):
+        return remote(unit(i), unit(i), sib_send.at[i], sib_recv.at[i], sib)
+
+    def from_sib(i):
+        return remote(out.at[1 - c, i], out.at[1 - c, i], sib_send.at[i], sib_recv.at[i], sib)
+
+    shards = list(enumerate((in_ref, go_ref)))
+    locals_ = [pltpu.make_async_copy(ref, out.at[a, z, c], loc.at[a]) for a, ref in shards]
+    owns = [remote(ref, out.at[a, z, c], own_send.at[a], own_recv.at[a], sib) for a, ref in shards]
+    for one in owns + locals_:
+        one.start()
+    for one in locals_:
+        one.wait()
+    for one in owns:
+        one.wait_recv()
+
+    def from_z(d, o, onward, near):
+        right(o).wait_recv()
+        if onward is not None:
+            onward(o)
+        if d == 1:
+
+            @pl.when(near)
+            def _():
+                to_x(o, 1 - r).start()
+                to_y(o, 1 - r).start()
+
+        to_sib(o).start()
+
+    def from_xy(i):
+        to_x(z, i).wait_recv()
+        pl.when(i == 0)(lambda: onward_y().start())
+        to_sib(zs + i).start()
+        to_y(z, i).wait_recv()
+        pl.when(i == 1)(lambda: onward_x().start())
+        to_sib(zs + 2 + i).start()
+
+    pl.when(z < zs - 1)(lambda: right(z).start())
+    pl.when(z > 0)(lambda: left(z).start())
+    to_x(z, r).start()
+    to_y(z, r).start()
+    for d in range(1, zs):
+
+        @pl.when(z - d >= 0)
+        def _(d=d):
+            def on(o):
+                pl.when(z < zs - 1)(lambda: right(o).start())
+
+            from_z(d, z - d, on, r == 1)
+
+        @pl.when(z + d < zs)
+        def _(d=d):
+            def on(o):
+                pl.when(z > 0)(lambda: left(o).start())
+
+            from_z(d, z + d, on, r == 0)
+
+        if d == 1:
+            from_xy(r)
+        if d == 2:
+            from_xy(1 - r)
+    onward_y().wait_recv()
+    to_sib(zs + 4).start()
+    onward_x().wait_recv()
+    to_sib(zs + 5).start()
+
+    for one in owns:
+        one.wait_send()
+    for o in range(zs):
+        pl.when((o <= z) & (z < zs - 1))(lambda o=o: right(o).wait_send())
+        pl.when((o >= z) & (z > 0))(lambda o=o: left(o).wait_send())
+
+        @pl.when(z != o)
+        def _(o=o):
+            to_sib(o).wait_send()
+            from_sib(o).wait_recv()
+
+    for i in range(2):
+        to_x(z, i).wait_send()
+        to_y(z, i).wait_send()
+    onward_y().wait_send()
+    onward_x().wait_send()
+    for i in range(zs, zs + 6):
+        to_sib(i).wait_send()
+        from_sib(i).wait_recv()
+
+
+def gather_first(inputs, grad_out, zs):
+    rows, features = inputs.shape
+    dma = pltpu.SemaphoreType.DMA
+    units = zs + 6
+    return pl.pallas_call(
+        functools.partial(gather_kernel, zs),
+        out_shape=jax.ShapeDtypeStruct((2, units, 2, rows, features), inputs.dtype),
+        in_specs=[pl.BlockSpec(memory_space=pl.ANY)] * 2,
+        out_specs=pl.BlockSpec(memory_space=pl.ANY),
+        scratch_shapes=[
+            dma((2,)),
+            dma((2,)),
+            dma((2,)),
+            dma((zs,)),
+            dma((2, zs)),
+            dma((3, 2)),
+            dma((3, 2)),
+            dma((units,)),
+            dma((units,)),
+        ],
+        compiler_params=pltpu.CompilerParams(collective_id=0, has_side_effects=True),
+        name="gather_first",
+    )(inputs, grad_out)
+
+
+def picked_blocks(ref, index, j, slots, width):
+    return jnp.concatenate(
+        [ref[:, pl.ds(pl.multiple_of(index[j, k] * width, width), width)] for k in range(slots)], axis=1
+    )
+
+
+def forward(xs, gs, up, down):
+    slots, width, _ = up.shape
+    preact = jnp.dot(xs, up.reshape(slots * width, width), preferred_element_type=jnp.float32)
+    down_wide = jnp.concatenate([down[k] for k in range(slots)], axis=1)
+    hidden_grad = lax.dot_general(
+        gs, down_wide, (((1,), (1,)), ((), ())), preferred_element_type=jnp.float32
+    )
+    gating = jax.nn.sigmoid(preact)
+    pg = (hidden_grad * gating * (1.0 + preact * (1.0 - gating))).astype(jnp.bfloat16)
+    return (preact * gating).astype(jnp.bfloat16), pg
+
+
+def input_kernel(ui, di, pos, x_ref, g_ref, up_ref, down_ref, out_ref, acc):
+    j = pl.program_id(0)
+    slots, width = up_ref.shape[1], up_ref.shape[2]
+
+    @pl.when(j == 0)
+    def _():
+        acc[...] = jnp.zeros_like(acc)
+
+    together = up_ref.shape[0]
+    terms = []
+    for u in range(together):
+        row = j * together + u
+        xs = picked_blocks(x_ref, ui, row, slots, width)
+        gs = picked_blocks(g_ref, di, row, slots, width)
+        up = up_ref[u]
+        _, pg = forward(xs, gs, up, down_ref[u])
+        terms.append(
+            lax.dot_general(
+                pg,
+                up.reshape(slots * width, width),
+                (((1,), (1,)), ((), ())),
+                preferred_element_type=jnp.float32,
+            )
+        )
+    for u in range(together):
+        for k in range(slots):
+            where = pl.ds(pl.multiple_of(ui[j * together + u, k] * width, width), width)
+            acc[:, where] += terms[u][:, k * width : (k + 1) * width]
+
+    @pl.when(j == pl.num_programs(0) - 1)
+    def _():
+        out_ref[...] = acc[...].astype(out_ref.dtype)
+
+
+def input_part(up_index, down_index, pos, both, up_blocks, down_blocks, rows):
+    count, slots, width, _ = up_blocks.shape
+    features = both.shape[2]
+    together = math.gcd(count, 4)
+    weight = pl.BlockSpec((together, slots, width, width), lambda j, *_: (j, 0, 0, 0))
+    return pl.pallas_call(
+        input_kernel,
+        out_shape=jax.ShapeDtypeStruct((rows, features), both.dtype),
+        grid_spec=pltpu.PrefetchScalarGridSpec(
+            num_scalar_prefetch=3,
+            grid=(count // together,),
+            in_specs=[
+                pl.BlockSpec(
+                    (None, rows, features), lambda j, *_: (0, 0, 0), pipeline_mode=pl.Buffered(1)
+                ),
+                pl.BlockSpec(
+                    (None, rows, features), lambda j, *_: (1, 0, 0), pipeline_mode=pl.Buffered(1)
+                ),
+                weight,
+                weight,
+            ],
+            out_specs=pl.BlockSpec((rows, features), lambda j, *_: (0, 0), pipeline_mode=pl.Buffered(1)),
+            scratch_shapes=[pltpu.VMEM((rows, features), jnp.float32)],
+        ),
+        compiler_params=pltpu.CompilerParams(vmem_limit_bytes=40 * MIB),
+        cost_estimate=pl.CostEstimate(
+            flops=6 * rows * count * slots * width * width,
+            bytes_accessed=4 * count * slots * width * width + 6 * rows * features,
+            transcendentals=rows * count * width,
+        ),
+        name="input_part",
+    )(up_index, down_index, pos, both, both, up_blocks, down_blocks)
+
+
+def grads_kernel(
+    factor, rows, first, ui, di, have, up_hbm, down_hbm, gup_ref, gdown_ref, far,
+    near_x, near_g, far_x, far_g, up, down, gup_acc, gdown_acc, near_xq, far_xq, near_turned, far_turned,
+    fill, near_fill, far_fill, send, recv, sib_send, sib_recv,
+):
+    s, t, z, c, xdev, ydev, sib = place()
+    count, slots, width, _ = up.shape
+    share = gup_ref.shape[2]
+    mine = pl.ds(pl.multiple_of(s * share, share), share)
+
+    barrier = pltpu.get_barrier_semaphore()
+    for dev in (sib, xdev, ydev):
+        pl.semaphore_signal(barrier, inc=1, device_id=dev, device_id_type=MESH)
+    pl.semaphore_wait(barrier, 3)
+
+    def piece(i):
+        return far.at[c, pl.ds(i * rows, rows)]
+
+    def held(i):
+        return have.at[c, pl.ds(pl.multiple_of((2 * (1 - z // 2) + i) * rows, rows), rows)]
+
+    def to_x(i):
+        return remote(held(i), piece(i), send.at[i], recv.at[i], xdev)
+
+    def to_y(i):
+        return remote(held(i), piece(2 + i), send.at[2 + i], recv.at[2 + i], ydev)
+
+    def onward_y():
+        return remote(piece(0), piece(4), send.at[4], recv.at[4], ydev)
+
+    def onward_x():
+        return remote(piece(3), piece(5), send.at[5], recv.at[5], xdev)
+
+    def to_sib(i):
+        return remote(piece(i), piece(i), sib_send.at[i], sib_recv.at[i], sib)
+
+    def from_sib(i):
+        other = far.at[1 - c, pl.ds(i * rows, rows)]
+        return remote(other, other, sib_send.at[i], sib_recv.at[i], sib)
+
+    sends = (to_x(0), to_x(1), to_y(0), to_y(1), onward_y(), onward_x())
+    for i in (0, 3, 1, 2):
+        sends[i].start()
+    fills = [
+        pltpu.make_async_copy(src, dst, fill.at[i])
+        for i, (src, dst) in enumerate(((up_hbm, up), (down_hbm, down)))
+    ]
+
+    def columns(src, a, dst, sems, b):
+        where = pl.ds(pl.multiple_of(b * width, width), width)
+        return pltpu.make_async_copy(src.at[a, :, where], dst.at[b], sems.at[a, b])
+
+    def start_columns(src, x, g, sems):
+        def one(b, carry):
+            columns(src, 0, x, sems, b).start()
+            columns(src, 1, g, sems, b).start()
+            return carry
+
+        lax.fori_loop(0, x.shape[0], one, 0)
+
+    def wait_columns(src, x, g, sems):
+        def one(b, carry):
+            columns(src, 0, x, sems, b).wait()
+            columns(src, 1, g, sems, b).wait()
+            return carry
+
+        lax.fori_loop(0, x.shape[0], one, 0)
+
+    start_columns(have, near_x, near_g, near_fill)
+    for one in fills:
+        one.start()
+
+    def arrived(i):
+        sends[i].wait_recv()
+
+    def turn(x, xq, turned):
+        together = turned.shape[0]
+
+        def one(b, carry):
+            for u in range(together):
+                block = b * together + u
+                turned[u] = x[block].T
+                xq[block] = turned[u, mine, :]
+            return carry
+
+        lax.fori_loop(0, xq.shape[0] // together, one, 0)
+
+    def add(x, g, xq, turned, start, stop, last):
+        together = turned.shape[0]
+
+        def one(j, carry):
+            for u in range(together):
+                row = j * together + u
+                xs = jnp.concatenate([x[ui[row, k]] for k in range(slots)], axis=1)
+                gs = jnp.concatenate([g[di[row, k]] for k in range(slots)], axis=1)
+                activated, pg = forward(xs, gs, up[row], down[row])
+                quarter = jnp.concatenate([xq[ui[row, k]] for k in range(slots)], axis=0)
+                gup = jnp.dot(quarter, pg, preferred_element_type=jnp.float32)
+                gup = gup.reshape(slots, share, width)
+                turned[u] = activated.T
+                gdown = jnp.dot(turned[u, mine, :], gs, preferred_element_type=jnp.float32)
+                if last:
+                    gup_ref[row] = ((gup_acc[row] + gup) * factor).astype(gup_ref.dtype)
+                else:
+                    gup_acc[row] = gup
+                for k in range(slots):
+                    part = gdown[:, k * width : (k + 1) * width]
+                    if last:
+                        gdown_ref[row, k] = ((gdown_acc[row, k] + part) * factor).astype(gdown_ref.dtype)
+                    else:
+                        gdown_acc[row, k] = part
+            return carry
+
+        lax.fori_loop(start // together, stop // together, one, 0)
+
+    wait_columns(have, near_x, near_g, near_fill)
+    turn(near_x, near_xq, near_turned)
+    for one in fills:
+        one.wait()
+    add(near_x, near_g, near_xq, near_turned, 0, first, False)
+    arrived(0)
+    sends[4].start()
+    to_sib(0).start()
+    arrived(3)
+    sends[5].start()
+    to_sib(3).start()
+    add(near_x, near_g, near_xq, near_turned, first, count, False)
+    for i in (1, 2, 4, 5):
+        arrived(i)
+        to_sib(i).start()
+    for i in range(6):
+        from_sib(i).wait_recv()
+    start_columns(far, far_x, far_g, far_fill)
+    wait_columns(far, far_x, far_g, far_fill)
+    turn(far_x, far_xq, far_turned)
+    add(far_x, far_g, far_xq, far_turned, 0, count, True)
+    for i in range(6):
+        sends[i].wait_send()
+        to_sib(i).wait_send()
+
+
+def block_grads(up_index, down_index, have, up_blocks, down_blocks, rows, share, factor):
+    count, slots, width, _ = up_blocks.shape
+    _, tokens, features = have.shape
+    dtype = have.dtype
+    together = math.gcd(count, 2)
+    first = count // 2 // together * together
+    blocks = features // width
+    shape = jax.ShapeDtypeStruct((count, slots, share, width), dtype)
+    dma = pltpu.SemaphoreType.DMA
+    vmem = pltpu.VMEM
+    return pl.pallas_call(
+        functools.partial(grads_kernel, factor, rows, first),
+        out_shape=[shape, shape, jax.ShapeDtypeStruct((2, 6 * rows, features), dtype)],
+        in_specs=[pl.BlockSpec(memory_space=pltpu.SMEM)] * 2 + [pl.BlockSpec(memory_space=pl.ANY)] * 3,
+        out_specs=[pl.BlockSpec(memory_space=vmem)] * 2 + [pl.BlockSpec(memory_space=pl.ANY)],
+        scratch_shapes=[
+            vmem((blocks, tokens, width), dtype),
+            vmem((blocks, tokens, width), dtype),
+            vmem((blocks, 6 * rows, width), dtype),
+            vmem((blocks, 6 * rows, width), dtype),
+            vmem(up_blocks.shape, dtype),
+            vmem(down_blocks.shape, dtype),
+            vmem(shape.shape, jnp.float32),
+            vmem(shape.shape, jnp.float32),
+            vmem((blocks, share, tokens), dtype),
+            vmem((blocks, share, 6 * rows), dtype),
+            vmem((together, width, tokens), dtype),
+            vmem((together, width, 6 * rows), dtype),
+            dma((2,)),
+            dma((2, blocks)),
+            dma((2, blocks)),
+            dma((6,)),
+            dma((6,)),
+            dma((6,)),
+            dma((6,)),
+        ],
+        compiler_params=pltpu.CompilerParams(
+            collective_id=1, has_side_effects=True, vmem_limit_bytes=61 * MIB
+        ),
+        cost_estimate=pl.CostEstimate(
+            flops=10 * tokens * count * slots * width * width,
+            bytes_accessed=6 * count * slots * width * width + 6 * tokens * features,
+            transcendentals=2 * tokens * count * width,
+        ),
+        name="block_grads",
+    )(up_index, down_index, have, up_blocks, down_blocks)
+
+
+def local_all_tokens(inputs, grad_out, up_blocks, up_index, down_blocks, down_index):
+    tensor_count = lax.axis_size("tensor")
+    seq_count = lax.axis_size("seq")
+    rows_here, features = inputs.shape
+    block = up_blocks.shape[2]
+    group_rows = rows_here * tensor_count
+    factor = 1.0 / math.sqrt(group_rows * seq_count)
+    have = gather_first(inputs, grad_out, tensor_count // 2)
+    have = have.reshape(2, -1, features)
+    pos = lax.axis_index("seq").astype(jnp.int32).reshape(1)
+    part = input_part(up_index, down_index, pos, have, up_blocks, down_blocks, group_rows)
+    pieces = part.reshape(tensor_count, rows_here, features)
+    received = lax.all_to_all(pieces, "tensor", split_axis=0, concat_axis=0, tiled=True)
+    grad_up, grad_down, _ = block_grads(
+        up_index, down_index, have, up_blocks, down_blocks, 2 * rows_here, block // seq_count, factor
+    )
+    grad_in = jnp.sum(received.astype(jnp.float32), axis=0).astype(jnp.bfloat16)
+    return (grad_in, grad_up, grad_down)
 
 
 def local(inputs, grad_out, up_blocks, up_index, down_blocks, down_index):
@@ -61,10 +530,10 @@
     grad_in = jnp.sum(received.astype(jnp.float32), axis=0).astype(jnp.bfloat16)
     return (grad_in, grad_up, grad_down)
 
-
 def solution(mesh):
+    gathers = mesh.shape["seq"] == 4 and mesh.shape["tensor"] == 8
     return jax.shard_map(
-        local,
+        local_all_tokens if gathers else local,
         mesh=mesh,
         in_specs=(
             P(("seq", "tensor"), None),

time: 402 us -> 220 us (0.55)
  Pallas kernels: 0 us -> 201 us
  waiting for transfers between devices: 183 us -> 0.01 us
  other arithmetic: 76.6 us -> 3.3 us
  local copies, waits for them, and re-layouts: 60.8 us -> 9.1 us
  matrix products: 50.8 us -> 0 us
  between operations: 14.2 us -> 0.7 us
  starting transfers between devices: 15.1 us -> 4.52 us
    pallas_call x0 -> x3, Pallas kernels: none -> 201 us  [the longest x1 90.7 us: block_grads(): pl.pallas_call(functools.partial(grads_kernel, factor, rows, first), out_...]
    all_to_all x3 -> x1, waiting for transfers between devices: 117 us -> 0.01 us  [local_all_tokens(): lax.all_to_all(pieces, 'tensor', split_axis=0, concat_axis=0, tiled=True)]
    all_gather x2 -> x0, waiting for transfers between devices: 64.6 us -> none  [the longest x1 38.6 us: local(): grad_rows = lax.all_gather(grad_out, 'tensor', axis=0, tiled=True)]
    scatter-add x1 -> x0, other arithmetic: 56.7 us -> none  [local(): jnp.zeros((piece_rows, blocks_wide, block), jnp.float32).at[:, flat_index]]
    dot_general x5 -> x0, matrix products: 50.8 us -> none  [the longest x1 13.4 us: local(): jnp.einsum('rjh,jkch->rjkc', preact_grad, up_blocks, preferred_element_ty...]
    gather x2 -> x0, local copies, waits for them, and re-layouts: 20.3 us -> none  [the longest x1 10.2 us: local(): jnp.take(in_rows.reshape(piece_rows, blocks_wide, block), up_index, axis=1)]
    reshape x5 -> x0, local copies, waits for them, and re-layouts: 19.3 us -> none  [the longest x1 8.38 us: local(): down_part = (down_sum * factor).astype(jnp.bfloat16).reshape(local_blocks...]
    convert_element_type x3 -> x0, local copies, waits for them, and re-layouts: 15.8 us -> none  [the longest x1 10.4 us: local(): down_part = (down_sum * factor).astype(jnp.bfloat16).reshape(local_blocks...]
  transfers between devices with their start and end apart: 5 -> 1, of which waited for: 4 -> 0; matrix products, arithmetic and copies ran while one was open for 34% -> 0% of each run, Pallas kernels for 0% -> 41%
where the time goes in v3:
time: 220 us; the launch traced here: 219 us
  Pallas kernels  201 us (91%)
  local copies, waits for them, and re-layouts  9.1 us (4%)
  starting transfers between devices  4.52 us (2%)
  other arithmetic  3.3 us (2%)
    pallas_call x1, Pallas kernels, block_grads(): pl.pallas_call(functools.partial(grads_kernel, factor, rows, first), out_...  90.7 us
    pallas_call x1, Pallas kernels, gather_first(): pl.pallas_call(functools.partial(gather_kernel, zs), out_shape=jax.ShapeD...  88.5 us
    pallas_call x1, Pallas kernels, input_part(): pl.pallas_call(input_kernel, out_shape=jax.ShapeDtypeStruct((rows, featur...  22.2 us
    unnamed x12, local copies, waits for them, and re-layouts  9.1 us
    all_to_all x1, starting transfers between devices, local_all_tokens(): lax.all_to_all(pieces, 'tensor', split_axis=0, concat_axis=0, tiled=True)  4.52 us
  transfers between devices with their start and end apart: 1, of which 0 were waited for; matrix products, arithmetic and copies ran while one was open for 0% of the time, Pallas kernels for 41%

profile of v3, /device:TPU:0, one launch (start us, length us, event | category | flops | bytes accessed | tf_op | source)
XLA Modules:
  0.0 219.0 jit_solution(6630468655982243306)
XLA Ops:
  0.6 0.8 copy.10.di
  1.4 0.0 copy-start.1
  1.4 0.8 copy.9.ui
  2.2 0.0 copy-start.2
  2.2 88.5 %gather_first.1 = bf16[2,10,2,24,8192]{4,3,2,1,0:T(8,128)(2,1)} custom-call(bf16[24,8192]{1,0:T(8,128)(2,1)} %in_ref.1, bf16[24,8192]{1,0:T(8,128)(2,1)} %go_ref.1), custom_call_target="tpu_custom_call" | custom-call | tf_op jit(solution)/shard_map/gather_first/pallas_call | solution.py:162
  90.7 0.0 copy-done.1
  90.7 0.0 copy-done.2
  90.7 0.0 copy-start
  90.7 3.1 %copy-done = bf16[28,8,128,128]{3,2,1,0:T(8,128)(2,1)S(1)} copy-done((bf16[28,8,128,128]{3,2,1,0:T(8,128)(2,1)S(1)}, bf16[28,8,128,128]{3,2,1,0:T(8,128)(2,1)}, u32[]{:S(2)}) %copy-start) | copy-done | bytes 7340056
  93.8 22.2 %input_part.1 = bf16[192,8192]{1,0:T(8,128)(2,1)} custom-call(s32[28,8]{1,0:T(8,128)S(1)} %copy.9.ui, s32[28,8]{1,0:T(8,128)S(1)} %copy.10.di, s32[1]{0:T(128)} %bitcast.pos, bf16[2,480,8192]{2,1,0:T(8,128)(2,1)} %bitcast.3, bf16[2,480,8192]{2,1,0:T(8,128)(2,1)} %bitcast.4, bf16[28,8,128,128]{3,2,1,0:T(8,128)(2,1)S(1)} %copy-done, ...), custom_call_target="tpu_custom_call" | custom-call | flops 4227858432 | bytes 24117248 | tf_op jit(solution)/shard_map/input_part/pallas_call | solution.py:240
  116.0 4.5 %all-to-all-start = ((bf16[8,24,8192]{2,1,0:T(8,128)(2,1)}), bf16[8,24,8192]{2,1,0:T(8,128)(2,1)}, u32[]{:S(2)}, u32[]{:S(2)}) async-start(bf16[8,24,8192]{2,1,0:T(8,128)(2,1)} %bitcast.2), calls=%async_computation | async-start | bytes 6291456 | tf_op jit(solution)/shard_map/all_to_all | solution.py:470
  120.5 90.7 %block_grads.1 = (bf16[28,8,32,128]{3,2,1,0:T(8,128)(2,1)}, bf16[28,8,32,128]{3,2,1,0:T(8,128)(2,1)}, bf16[2,288,8192]{2,1,0:T(8,128)(2,1)}) custom-call(s32[28,8]{1,0:T(8,128)} %copy-done.2, s32[28,8]{1,0:T(8,128)} %copy-done.1, bf16[2,480,8192]{2,1,0:T(8,128)(2,1)} %bitcast.5, bf16[28,8,128,128]{3,2,1,0:T(8,128)(2,1)} %up_hbm.1, ...), custom_call_target="tpu_custom_call" | custom-call | flops 17616076800 | bytes 45613056 | tf_op jit(solution)/shard_map/block_grads/pallas_call | solution.py:420
  211.2 0.0 copy-start.3
  211.2 0.0 all-to-all-done
  211.2 3.3 %reduce_sum.12 = bf16[24,8192]{1,0:T(8,128)(2,1)} reduce(bf16[8,24,8192]{2,1,0:T(8,128)(2,1)} %all-to-all-done, bf16[]{:T(256)} %constant.7.clone.1), dimensions={0}, to_apply=%region_0.0 | reduce | flops 1376256 | bytes 3538946 | tf_op jit(solution)/shard_map/reduce_sum | solution.py:474
  214.5 3.2 %copy.15 = bf16[28,8,32,128]{3,2,1,0:T(8,128)(2,1)} copy(bf16[28,8,32,128]{3,2,1,0:T(8,128)(2,1)} %get-tuple-element.11) | data formatting | bytes 3670016
  217.7 0.0 copy-done.3
  217.7 1.2 copy.16
Async XLA Ops:
  1.4 89.3 %copy-start.1 = (s32[28,8]{1,0:T(8,128)}, s32[28,8]{1,0:T(8,128)S(1)}, u32[]{:S(2)}) copy-start(s32[28,8]{1,0:T(8,128)S(1)} %copy.10.di) | copy-start | bytes 2692
  2.2 88.5 %copy-start.2 = (s32[28,8]{1,0:T(8,128)}, s32[28,8]{1,0:T(8,128)S(1)}, u32[]{:S(2)}) copy-start(s32[28,8]{1,0:T(8,128)S(1)} %copy.9.ui) | copy-start | bytes 2692
  90.7 3.1 %copy-start = (bf16[28,8,128,128]{3,2,1,0:T(8,128)(2,1)S(1)}, bf16[28,8,128,128]{3,2,1,0:T(8,128)(2,1)}, u32[]{:S(2)}) copy-start(bf16[28,8,128,128]{3,2,1,0:T(8,128)(2,1)} %up_hbm.1) | copy-start | bytes 22020100
  116.0 95.2 %all-to-all-start = ((bf16[8,24,8192]{2,1,0:T(8,128)(2,1)}), bf16[8,24,8192]{2,1,0:T(8,128)(2,1)}, u32[]{:S(2)}, u32[]{:S(2)}) async-start(bf16[8,24,8192]{2,1,0:T(8,128)(2,1)} %bitcast.2), calls=%async_computation | async-start | bytes 6291456 | tf_op jit(solution)/shard_map/all_to_all | solution.py:470
  211.2 6.5 %copy-start.3 = (bf16[28,8,32,128]{3,2,1,0:T(8,128)(2,1)S(1)}, bf16[28,8,32,128]{3,2,1,0:T(8,128)(2,1)}, u32[]{:S(2)}) copy-start(bf16[28,8,32,128]{3,2,1,0:T(8,128)(2,1)} %get-tuple-element.12) | copy-start | bytes 5505028

commit v4 on v3

--- a/solution.py
+++ b/solution.py
@@ -68,11 +68,26 @@
     def onward_x():
         return remote(unit(zs + 3), unit(zs + 5), send.at[2, 1], recv.at[2, 1], xdev)
 
+    parts = sib_send.shape[1] // 2
+    wide = in_ref.shape[1] // parts
+
+    def with_sib(a, i):
+        refs = [out.at[a, i, h, :, pl.ds(f * wide, wide)] for h in range(2) for f in range(parts)]
+        return [
+            remote(ref, ref, sib_send.at[i, n], sib_recv.at[i, n], sib) for n, ref in enumerate(refs)
+        ]
+
     def to_sib(i):
-        return remote(unit(i), unit(i), sib_send.at[i], sib_recv.at[i], sib)
+        for one in with_sib(c, i):
+            one.start()
+
+    def sent_sib(i):
+        for one in with_sib(c, i):
+            one.wait_send()
 
     def from_sib(i):
-        return remote(out.at[1 - c, i], out.at[1 - c, i], sib_send.at[i], sib_recv.at[i], sib)
+        for one in with_sib(1 - c, i):
+            one.wait_recv()
 
     shards = list(enumerate((in_ref, go_ref)))
     locals_ = [pltpu.make_async_copy(ref, out.at[a, z, c], loc.at[a]) for a, ref in shards]
@@ -95,15 +110,15 @@
                 to_x(o, 1 - r).start()
                 to_y(o, 1 - r).start()
 
-        to_sib(o).start()
+        to_sib(o)
 
     def from_xy(i):
         to_x(z, i).wait_recv()
         pl.when(i == 0)(lambda: onward_y().start())
-        to_sib(zs + i).start()
+        to_sib(zs + i)
         to_y(z, i).wait_recv()
         pl.when(i == 1)(lambda: onward_x().start())
-        to_sib(zs + 2 + i).start()
+        to_sib(zs + 2 + i)
 
     pl.when(z < zs - 1)(lambda: right(z).start())
     pl.when(z > 0)(lambda: left(z).start())
@@ -130,9 +145,9 @@
         if d == 2:
             from_xy(1 - r)
     onward_y().wait_recv()
-    to_sib(zs + 4).start()
+    to_sib(zs + 4)
     onward_x().wait_recv()
-    to_sib(zs + 5).start()
+    to_sib(zs + 5)
 
     for one in owns:
         one.wait_send()
@@ -142,8 +157,8 @@
 
         @pl.when(z != o)
         def _(o=o):
-            to_sib(o).wait_send()
-            from_sib(o).wait_recv()
+            sent_sib(o)
+            from_sib(o)
 
     for i in range(2):
         to_x(z, i).wait_send()
@@ -151,8 +166,8 @@
     onward_y().wait_send()
     onward_x().wait_send()
     for i in range(zs, zs + 6):
-        to_sib(i).wait_send()
-        from_sib(i).wait_recv()
+        sent_sib(i)
+        from_sib(i)
 
 
 def gather_first(inputs, grad_out, zs):
@@ -172,8 +187,8 @@
             dma((2, zs)),
             dma((3, 2)),
             dma((3, 2)),
-            dma((units,)),
-            dma((units,)),
+            dma((units, 4)),
+            dma((units, 4)),
         ],
         compiler_params=pltpu.CompilerParams(collective_id=0, has_side_effects=True),
         name="gather_first",
@@ -256,7 +271,7 @@
             out_specs=pl.BlockSpec((rows, features), lambda j, *_: (0, 0), pipeline_mode=pl.Buffered(1)),
             scratch_shapes=[pltpu.VMEM((rows, features), jnp.float32)],
         ),
-        compiler_params=pltpu.CompilerParams(vmem_limit_bytes=40 * MIB),
+        compiler_params=pltpu.CompilerParams(vmem_limit_bytes=60 * MIB),
         cost_estimate=pl.CostEstimate(
             flops=6 * rows * count * slots * width * width,
             bytes_accessed=4 * count * slots * width * width + 6 * rows * features,
@@ -411,7 +426,7 @@
     count, slots, width, _ = up_blocks.shape
     _, tokens, features = have.shape
     dtype = have.dtype
-    together = math.gcd(count, 2)
+    together = math.gcd(count, 4)
     first = count // 2 // together * together
     blocks = features // width
     shape = jax.ShapeDtypeStruct((count, slots, share, width), dtype)

time: 220 us -> 218 us (level)
    unnamed x12 -> x6, local copies, waits for them, and re-layouts: 9.1 us -> 7.2 us
where the time goes in v4:
time: 218 us; the launch traced here: 216 us
  Pallas kernels  201 us (92%)
  local copies, waits for them, and re-layouts  7.2 us (3%)
  starting transfers between devices  4.68 us (2%)
  other arithmetic  3.3 us (2%)
    pallas_call x1, Pallas kernels, block_grads(): pl.pallas_call(functools.partial(grads_kernel, factor, rows, first), out_...  89 us
    pallas_call x1, Pallas kernels, gather_first(): pl.pallas_call(functools.partial(gather_kernel, zs), out_shape=jax.ShapeD...  89 us
    pallas_call x1, Pallas kernels, input_part(): pl.pallas_call(input_kernel, out_shape=jax.ShapeDtypeStruct((rows, featur...  22.6 us
    unnamed x6, local copies, waits for them, and re-layouts  7.2 us
    all_to_all x1, starting transfers between devices, local_all_tokens(): lax.all_to_all(pieces, 'tensor', split_axis=0, concat_axis=0, tiled=True)  4.68 us
  transfers between devices with their start and end apart: 1, of which 0 were waited for; matrix products, arithmetic and copies ran while one was open for 0% of the time, Pallas kernels for 41%

profile of v4, /device:TPU:0, one launch (start us, length us, event | category | flops | bytes accessed | tf_op | source)
XLA Modules:
  0.0 216.5 jit_solution(18308133612944606334)
XLA Ops:
  0.6 1.4 copy.10.di
  2.0 1.4 copy.9.ui
  3.4 89.0 %gather_first.1 = bf16[2,10,2,24,8192]{4,3,2,1,0:T(8,128)(2,1)} custom-call(bf16[24,8192]{1,0:T(8,128)(2,1)} %in_ref.1, bf16[24,8192]{1,0:T(8,128)(2,1)} %go_ref.1), custom_call_target="tpu_custom_call" | custom-call | tf_op jit(solution)/shard_map/gather_first/pallas_call | solution.py:177
  92.4 22.6 %input_part.1 = bf16[192,8192]{1,0:T(8,128)(2,1)} custom-call(s32[28,8]{1,0:T(8,128)} %copy.9.ui, s32[28,8]{1,0:T(8,128)} %copy.10.di, s32[1]{0:T(128)} %bitcast.pos, bf16[2,480,8192]{2,1,0:T(8,128)(2,1)} %bitcast.3, bf16[2,480,8192]{2,1,0:T(8,128)(2,1)} %bitcast.4, bf16[28,8,128,128]{3,2,1,0:T(8,128)(2,1)} %up_hbm.1, bf16[28,8,128,128]{3,2,1,0:T(8,128)(2,1)} %down_hbm.1), custom_call_target="tpu_custom_call" | custom-call | flops 4227858432 | bytes 24117248 | tf_op jit(solution)/shard_map/input_part/pallas_call | solution.py:255
  115.0 4.7 %all-to-all-start = ((bf16[8,24,8192]{2,1,0:T(8,128)(2,1)}), bf16[8,24,8192]{2,1,0:T(8,128)(2,1)}, u32[]{:S(2)}, u32[]{:S(2)}) async-start(bf16[8,24,8192]{2,1,0:T(8,128)(2,1)} %bitcast.6), calls=%async_computation | async-start | bytes 6291456 | tf_op jit(solution)/shard_map/all_to_all | solution.py:485
  119.7 89.0 %block_grads.1 = (bf16[28,8,32,128]{3,2,1,0:T(8,128)(2,1)}, bf16[28,8,32,128]{3,2,1,0:T(8,128)(2,1)}, bf16[2,288,8192]{2,1,0:T(8,128)(2,1)}) custom-call(s32[28,8]{1,0:T(8,128)} %copy.9.ui, s32[28,8]{1,0:T(8,128)} %copy.10.di, bf16[2,480,8192]{2,1,0:T(8,128)(2,1)} %bitcast.5, bf16[28,8,128,128]{3,2,1,0:T(8,128)(2,1)} %up_hbm.1, ...), custom_call_target="tpu_custom_call" | custom-call | flops 17616076800 | bytes 45613056 | tf_op jit(solution)/shard_map/block_grads/pallas_call | solution.py:435
  208.7 0.0 copy-start
  208.7 0.0 all-to-all-done
  208.7 3.3 %reduce_sum.12 = bf16[24,8192]{1,0:T(8,128)(2,1)} reduce(bf16[8,24,8192]{2,1,0:T(8,128)(2,1)} %all-to-all-done, bf16[]{:T(256)} %constant.7.clone.1), dimensions={0}, to_apply=%region_0.0 | reduce | flops 1376256 | bytes 3538946 | tf_op jit(solution)/shard_map/reduce_sum | solution.py:489
  212.0 3.2 %copy.15 = bf16[28,8,32,128]{3,2,1,0:T(8,128)(2,1)} copy(bf16[28,8,32,128]{3,2,1,0:T(8,128)(2,1)} %get-tuple-element.11) | data formatting | bytes 3670016
  215.3 0.0 copy-done
  215.3 1.2 copy.16
Async XLA Ops:
  115.0 93.7 %all-to-all-start = ((bf16[8,24,8192]{2,1,0:T(8,128)(2,1)}), bf16[8,24,8192]{2,1,0:T(8,128)(2,1)}, u32[]{:S(2)}, u32[]{:S(2)}) async-start(bf16[8,24,8192]{2,1,0:T(8,128)(2,1)} %bitcast.6), calls=%async_computation | async-start | bytes 6291456 | tf_op jit(solution)/shard_map/all_to_all | solution.py:485
  208.7 6.5 %copy-start = (bf16[28,8,32,128]{3,2,1,0:T(8,128)(2,1)S(1)}, bf16[28,8,32,128]{3,2,1,0:T(8,128)(2,1)}, u32[]{:S(2)}) copy-start(bf16[28,8,32,128]{3,2,1,0:T(8,128)(2,1)} %get-tuple-element.12) | copy-start | bytes 5505028

commit v5 on v4

--- a/solution.py
+++ b/solution.py
@@ -50,11 +50,11 @@
     def unit(i):
         return out.at[c, i]
 
-    def right(o):
-        return remote(unit(o), unit(o), zsend.at[0, o], zrecv.at[o], (s, t + 2))
-
-    def left(o):
-        return remote(unit(o), unit(o), zsend.at[1, o], zrecv.at[o], (s, t - 2))
+    def right(o, h):
+        return remote(out.at[c, o, h], out.at[c, o, h], zsend.at[0, o, h], zrecv.at[o, h], (s, t + 2))
+
+    def left(o, h):
+        return remote(out.at[c, o, h], out.at[c, o, h], zsend.at[1, o, h], zrecv.at[o, h], (s, t - 2))
 
     def to_x(o, i):
         return remote(unit(o), unit(zs + i), send.at[0, i], recv.at[0, i], xdev)
@@ -100,9 +100,9 @@
         one.wait_recv()
 
     def from_z(d, o, onward, near):
-        right(o).wait_recv()
-        if onward is not None:
-            onward(o)
+        for h in range(2):
+            right(o, h).wait_recv()
+            onward(o, h)
         if d == 1:
 
             @pl.when(near)
@@ -120,23 +120,24 @@
         pl.when(i == 1)(lambda: onward_x().start())
         to_sib(zs + 2 + i)
 
-    pl.when(z < zs - 1)(lambda: right(z).start())
-    pl.when(z > 0)(lambda: left(z).start())
+    for h in range(2):
+        pl.when(z < zs - 1)(lambda h=h: right(z, h).start())
+        pl.when(z > 0)(lambda h=h: left(z, h).start())
     to_x(z, r).start()
     to_y(z, r).start()
     for d in range(1, zs):
 
         @pl.when(z - d >= 0)
         def _(d=d):
-            def on(o):
-                pl.when(z < zs - 1)(lambda: right(o).start())
+            def on(o, h):
+                pl.when(z < zs - 1)(lambda: right(o, h).start())
 
             from_z(d, z - d, on, r == 1)
 
         @pl.when(z + d < zs)
         def _(d=d):
-            def on(o):
-                pl.when(z > 0)(lambda: left(o).start())
+            def on(o, h):
+                pl.when(z > 0)(lambda: left(o, h).start())
 
             from_z(d, z + d, on, r == 0)
 
@@ -152,8 +153,9 @@
     for one in owns:
         one.wait_send()
     for o in range(zs):
-        pl.when((o <= z) & (z < zs - 1))(lambda o=o: right(o).wait_send())
-        pl.when((o >= z) & (z > 0))(lambda o=o: left(o).wait_send())
+        for h in range(2):
+            pl.when((o <= z) & (z < zs - 1))(lambda o=o, h=h: right(o, h).wait_send())
+            pl.when((o >= z) & (z > 0))(lambda o=o, h=h: left(o, h).wait_send())
 
         @pl.when(z != o)
         def _(o=o):
@@ -183,8 +185,8 @@
             dma((2,)),
             dma((2,)),
             dma((2,)),
-            dma((zs,)),
-            dma((2, zs)),
+            dma((zs, 2)),
+            dma((2, zs, 2)),
             dma((3, 2)),
             dma((3, 2)),
             dma((units, 4)),
@@ -282,9 +284,8 @@
 
 
 def grads_kernel(
-    factor, rows, first, ui, di, have, up_hbm, down_hbm, gup_ref, gdown_ref, far,
-    near_x, near_g, far_x, far_g, up, down, gup_acc, gdown_acc, near_xq, far_xq, near_turned, far_turned,
-    fill, near_fill, far_fill, send, recv, sib_send, sib_recv,
+    rows, first, ui, di, have, up_hbm, down_hbm, gup_ref, gdown_ref, far,
+    near_x, near_g, up, down, near_xq, near_turned, fill, near_fill, send, recv, sib_send, sib_recv,
 ):
     s, t, z, c, xdev, ydev, sib = place()
     count, slots, width, _ = up.shape
@@ -368,7 +369,7 @@
 
         lax.fori_loop(0, xq.shape[0] // together, one, 0)
 
-    def add(x, g, xq, turned, start, stop, last):
+    def add(x, g, xq, turned, start, stop):
         together = turned.shape[0]
 
         def one(j, carry):
@@ -379,19 +380,11 @@
                 activated, pg = forward(xs, gs, up[row], down[row])
                 quarter = jnp.concatenate([xq[ui[row, k]] for k in range(slots)], axis=0)
                 gup = jnp.dot(quarter, pg, preferred_element_type=jnp.float32)
-                gup = gup.reshape(slots, share, width)
+                gup_ref[row] = gup.reshape(slots, share, width)
                 turned[u] = activated.T
                 gdown = jnp.dot(turned[u, mine, :], gs, preferred_element_type=jnp.float32)
-                if last:
-                    gup_ref[row] = ((gup_acc[row] + gup) * factor).astype(gup_ref.dtype)
-                else:
-                    gup_acc[row] = gup
                 for k in range(slots):
-                    part = gdown[:, k * width : (k + 1) * width]
-                    if last:
-                        gdown_ref[row, k] = ((gdown_acc[row, k] + part) * factor).astype(gdown_ref.dtype)
-                    else:
-                        gdown_acc[row, k] = part
+                    gdown_ref[row, k] = gdown[:, k * width : (k + 1) * width]
             return carry
 
         lax.fori_loop(start // together, stop // together, one, 0)
@@ -400,58 +393,47 @@
     turn(near_x, near_xq, near_turned)
     for one in fills:
         one.wait()
-    add(near_x, near_g, near_xq, near_turned, 0, first, False)
+    add(near_x, near_g, near_xq, near_turned, 0, first)
     arrived(0)
     sends[4].start()
     to_sib(0).start()
     arrived(3)
     sends[5].start()
     to_sib(3).start()
-    add(near_x, near_g, near_xq, near_turned, first, count, False)
+    add(near_x, near_g, near_xq, near_turned, first, count)
     for i in (1, 2, 4, 5):
         arrived(i)
         to_sib(i).start()
     for i in range(6):
         from_sib(i).wait_recv()
-    start_columns(far, far_x, far_g, far_fill)
-    wait_columns(far, far_x, far_g, far_fill)
-    turn(far_x, far_xq, far_turned)
-    add(far_x, far_g, far_xq, far_turned, 0, count, True)
     for i in range(6):
         sends[i].wait_send()
         to_sib(i).wait_send()
 
 
-def block_grads(up_index, down_index, have, up_blocks, down_blocks, rows, share, factor):
+def near_grads(up_index, down_index, have, up_blocks, down_blocks, rows, share):
     count, slots, width, _ = up_blocks.shape
     _, tokens, features = have.shape
     dtype = have.dtype
     together = math.gcd(count, 4)
     first = count // 2 // together * together
     blocks = features // width
-    shape = jax.ShapeDtypeStruct((count, slots, share, width), dtype)
+    shape = jax.ShapeDtypeStruct((count, slots, share, width), jnp.float32)
     dma = pltpu.SemaphoreType.DMA
     vmem = pltpu.VMEM
     return pl.pallas_call(
-        functools.partial(grads_kernel, factor, rows, first),
+        functools.partial(grads_kernel, rows, first),
         out_shape=[shape, shape, jax.ShapeDtypeStruct((2, 6 * rows, features), dtype)],
         in_specs=[pl.BlockSpec(memory_space=pltpu.SMEM)] * 2 + [pl.BlockSpec(memory_space=pl.ANY)] * 3,
         out_specs=[pl.BlockSpec(memory_space=vmem)] * 2 + [pl.BlockSpec(memory_space=pl.ANY)],
         scratch_shapes=[
             vmem((blocks, tokens, width), dtype),
             vmem((blocks, tokens, width), dtype),
-            vmem((blocks, 6 * rows, width), dtype),
-            vmem((blocks, 6 * rows, width), dtype),
             vmem(up_blocks.shape, dtype),
             vmem(down_blocks.shape, dtype),
-            vmem(shape.shape, jnp.float32),
-            vmem(shape.shape, jnp.float32),
             vmem((blocks, share, tokens), dtype),
-            vmem((blocks, share, 6 * rows), dtype),
             vmem((together, width, tokens), dtype),
-            vmem((together, width, 6 * rows), dtype),
             dma((2,)),
-            dma((2, blocks)),
             dma((2, blocks)),
             dma((6,)),
             dma((6,)),
@@ -459,15 +441,88 @@
             dma((6,)),
         ],
         compiler_params=pltpu.CompilerParams(
-            collective_id=1, has_side_effects=True, vmem_limit_bytes=61 * MIB
+            collective_id=1, has_side_effects=True, vmem_limit_bytes=60 * MIB
         ),
         cost_estimate=pl.CostEstimate(
-            flops=10 * tokens * count * slots * width * width,
+            flops=6 * tokens * count * slots * width * width,
             bytes_accessed=6 * count * slots * width * width + 6 * tokens * features,
-            transcendentals=2 * tokens * count * width,
-        ),
-        name="block_grads",
+            transcendentals=tokens * count * width,
+        ),
+        name="near_grads",
     )(up_index, down_index, have, up_blocks, down_blocks)
+
+
+def far_kernel(
+    factor, ui, di, pos, x_ref, g_ref, up_ref, down_ref, gup_in, gdown_in, gup_ref, gdown_ref, xq, turned
+):
+    j = pl.program_id(0)
+    together, slots, width, _ = up_ref.shape
+    share = gup_ref.shape[2]
+    mine = pl.ds(pl.multiple_of(pos[0] * share, share), share)
+
+    @pl.when(j == 0)
+    def _():
+        def one(b, carry):
+            for u in range(together):
+                block = b * together + u
+                turned[u] = x_ref[:, pl.ds(pl.multiple_of(block * width, width), width)].T
+                xq[block] = turned[u, mine, :]
+            return carry
+
+        lax.fori_loop(0, xq.shape[0] // together, one, 0)
+
+    for u in range(together):
+        row = j * together + u
+        xs = picked_blocks(x_ref, ui, row, slots, width)
+        gs = picked_blocks(g_ref, di, row, slots, width)
+        activated, pg = forward(xs, gs, up_ref[u], down_ref[u])
+        quarter = jnp.concatenate([xq[ui[row, k]] for k in range(slots)], axis=0)
+        gup = jnp.dot(quarter, pg, preferred_element_type=jnp.float32).reshape(slots, share, width)
+        gup_ref[u] = ((gup_in[u] + gup) * factor).astype(gup_ref.dtype)
+        turned[u] = activated.T
+        gdown = jnp.dot(turned[u, mine, :], gs, preferred_element_type=jnp.float32)
+        for k in range(slots):
+            part = gdown[:, k * width : (k + 1) * width]
+            gdown_ref[u, k] = ((gdown_in[u, k] + part) * factor).astype(gdown_ref.dtype)
+
+
+def far_grads(up_index, down_index, pos, far, up_blocks, down_blocks, gup, gdown, factor):
+    count, slots, width, _ = up_blocks.shape
+    share = gup.shape[2]
+    _, tokens, features = far.shape
+    together = math.gcd(count, 4)
+    weight = pl.BlockSpec((together, slots, width, width), lambda j, *_: (j, 0, 0, 0))
+    result = pl.BlockSpec((together, slots, share, width), lambda j, *_: (j, 0, 0, 0))
+    shape = jax.ShapeDtypeStruct((count, slots, share, width), far.dtype)
+    once = pl.Buffered(1)
+    return pl.pallas_call(
+        functools.partial(far_kernel, factor),
+        out_shape=[shape, shape],
+        grid_spec=pltpu.PrefetchScalarGridSpec(
+            num_scalar_prefetch=3,
+            grid=(count // together,),
+            in_specs=[
+                pl.BlockSpec((None, tokens, features), lambda j, *_: (0, 0, 0), pipeline_mode=once),
+                pl.BlockSpec((None, tokens, features), lambda j, *_: (1, 0, 0), pipeline_mode=once),
+                weight,
+                weight,
+                result,
+                result,
+            ],
+            out_specs=[result, result],
+            scratch_shapes=[
+                pltpu.VMEM((features // width, share, tokens), far.dtype),
+                pltpu.VMEM((together, width, tokens), far.dtype),
+            ],
+        ),
+        compiler_params=pltpu.CompilerParams(vmem_limit_bytes=60 * MIB),
+        cost_estimate=pl.CostEstimate(
+            flops=6 * tokens * count * slots * width * width,
+            bytes_accessed=6 * count * slots * width * width + 4 * tokens * features,
+            transcendentals=tokens * count * width,
+        ),
+        name="far_grads",
+    )(up_index, down_index, pos, far, far, up_blocks, down_blocks, gup, gdown)
 
 
 def local_all_tokens(inputs, grad_out, up_blocks, up_index, down_blocks, down_index):
@@ -483,8 +538,11 @@
     part = input_part(up_index, down_index, pos, have, up_blocks, down_blocks, group_rows)
     pieces = part.reshape(tensor_count, rows_here, features)
     received = lax.all_to_all(pieces, "tensor", split_axis=0, concat_axis=0, tiled=True)
-    grad_up, grad_down, _ = block_grads(
-        up_index, down_index, have, up_blocks, down_blocks, 2 * rows_here, block // seq_count, factor
+    near_up, near_down, far = near_grads(
+        up_index, down_index, have, up_blocks, down_blocks, 2 * rows_here, block // seq_count
+    )
+    grad_up, grad_down = far_grads(
+        up_index, down_index, pos, far, up_blocks, down_blocks, near_up, near_down, factor
     )
     grad_in = jnp.sum(received.astype(jnp.float32), axis=0).astype(jnp.bfloat16)
     return (grad_in, grad_up, grad_down)

time: 218 us -> 212 us (0.972)
  local copies, waits for them, and re-layouts: 7.2 us -> 2.74 us
    unnamed x6 -> x2, local copies, waits for them, and re-layouts: 7.2 us -> 2.74 us
    pallas_call x1 -> x2, Pallas kernels: 89 us -> 92.9 us  [the longest x1 63.7 us: near_grads(): pl.pallas_call(functools.partial(grads_kernel, rows, first), out_shape=[s...]
  transfers between devices with their start and end apart: 1 -> 1, of which waited for: 0 -> 0; matrix products, arithmetic and copies ran while one was open for 0% -> 0% of each run, Pallas kernels for 41% -> 44%
where the time goes in v5:
time: 212 us; the launch traced here: 211 us
  Pallas kernels  202 us (95%)
  starting transfers between devices  3.83 us (2%)
  local copies, waits for them, and re-layouts  2.74 us (1%)
    pallas_call x1, Pallas kernels, gather_first(): pl.pallas_call(functools.partial(gather_kernel, zs), out_shape=jax.ShapeD...  87 us
    pallas_call x1, Pallas kernels, near_grads(): pl.pallas_call(functools.partial(grads_kernel, rows, first), out_shape=[s...  63.7 us
    pallas_call x1, Pallas kernels, far_grads(): pl.pallas_call(functools.partial(far_kernel, factor), out_shape=[shape, s...  29.2 us
    pallas_call x1, Pallas kernels, input_part(): pl.pallas_call(input_kernel, out_shape=jax.ShapeDtypeStruct((rows, featur...  22.5 us
  transfers between devices with their start and end apart: 1, of which 0 were waited for; matrix products, arithmetic and copies ran while one was open for 0% of the time, Pallas kernels for 44%

profile of v5, /device:TPU:0, one launch (start us, length us, event | category | flops | bytes accessed | tf_op | source)
XLA Modules:
  0.0 211.0 jit_solution(8361663273549888870)
XLA Ops:
  0.6 1.4 copy.9.ui
  2.0 1.4 copy.10.di
  3.4 87.0 %gather_first.1 = bf16[2,10,2,24,8192]{4,3,2,1,0:T(8,128)(2,1)} custom-call(bf16[24,8192]{1,0:T(8,128)(2,1)} %in_ref.1, bf16[24,8192]{1,0:T(8,128)(2,1)} %go_ref.1), custom_call_target="tpu_custom_call" | custom-call | tf_op jit(solution)/shard_map/gather_first/pallas_call | solution.py:179
  90.4 22.5 %input_part.1 = bf16[192,8192]{1,0:T(8,128)(2,1)} custom-call(s32[28,8]{1,0:T(8,128)} %copy.9.ui, s32[28,8]{1,0:T(8,128)} %copy.10.di, s32[1]{0:T(128)} %bitcast.pos, bf16[2,480,8192]{2,1,0:T(8,128)(2,1)} %bitcast.3, bf16[2,480,8192]{2,1,0:T(8,128)(2,1)} %bitcast.4, bf16[28,8,128,128]{3,2,1,0:T(8,128)(2,1)} %up_ref.3, bf16[28,8,128,128]{3,2,1,0:T(8,128)(2,1)} %down_ref.3), custom_call_target="tpu_custom_call" | custom-call | flops 4227858432 | bytes 24117248 | tf_op jit(solution)/shard_map/input_part/pallas_call | solution.py:257
  112.9 3.8 %all-to-all-start = ((bf16[8,24,8192]{2,1,0:T(8,128)(2,1)}), bf16[8,24,8192]{2,1,0:T(8,128)(2,1)S(1)}, u32[]{:S(2)}, u32[]{:S(2)}) async-start(bf16[8,24,8192]{2,1,0:T(8,128)(2,1)} %bitcast.6), calls=%async_computation | async-start | bytes 6291456 | tf_op jit(solution)/shard_map/all_to_all | solution.py:540
  116.8 63.7 %near_grads.1 = (f32[28,8,32,128]{3,2,1,0:T(8,128)}, f32[28,8,32,128]{3,2,1,0:T(8,128)}, bf16[2,288,8192]{2,1,0:T(8,128)(2,1)}) custom-call(s32[28,8]{1,0:T(8,128)} %copy.9.ui, s32[28,8]{1,0:T(8,128)} %copy.10.di, bf16[2,480,8192]{2,1,0:T(8,128)(2,1)} %bitcast.5, bf16[28,8,128,128]{3,2,1,0:T(8,128)(2,1)} %up_ref.3, bf16[28,8,128,128]{3,2,1,0:T(8,128)(2,1)} %down_ref.3), custom_call_target="tpu_custom_call" | custom-call | flops 10569646080 | bytes 45613056 | tf_op jit(solution)/shard_map/near_grads/pallas_call | solution.py:424
  180.5 29.2 %far_grads.1 = (bf16[28,8,32,128]{3,2,1,0:T(8,128)(2,1)}, bf16[28,8,32,128]{3,2,1,0:T(8,128)(2,1)}) custom-call(s32[28,8]{1,0:T(8,128)} %copy.9.ui, s32[28,8]{1,0:T(8,128)} %copy.10.di, s32[1]{0:T(128)} %bitcast.pos, bf16[2,288,8192]{2,1,0:T(8,128)(2,1)} %get-tuple-element.8.x_ref.g_ref, bf16[2,288,8192]{2,1,0:T(8,128)(2,1)} %get-tuple-element.8.x_ref.g_ref, ...), custom_call_target="tpu_custom_call" | custom-call | flops 6341787648 | bytes 31457280 | tf_op jit(solution)/shard_map/far_grads/pallas_call | solution.py:498
  209.7 0.0 all-to-all-done
  209.7 1.3 reduce_sum.12
Async XLA Ops:
  112.9 96.8 %all-to-all-start = ((bf16[8,24,8192]{2,1,0:T(8,128)(2,1)}), bf16[8,24,8192]{2,1,0:T(8,128)(2,1)S(1)}, u32[]{:S(2)}, u32[]{:S(2)}) async-start(bf16[8,24,8192]{2,1,0:T(8,128)(2,1)} %bitcast.6), calls=%async_computation | async-start | bytes 6291456 | tf_op jit(solution)/shard_map/all_to_all | solution.py:540

commit v6 on v5

--- a/solution.py
+++ b/solution.py
@@ -323,7 +323,7 @@
         return remote(other, other, sib_send.at[i], sib_recv.at[i], sib)
 
     sends = (to_x(0), to_x(1), to_y(0), to_y(1), onward_y(), onward_x())
-    for i in (0, 3, 1, 2):
+    for i in (0, 3):
         sends[i].start()
     fills = [
         pltpu.make_async_copy(src, dst, fill.at[i])
@@ -390,6 +390,8 @@
         lax.fori_loop(start // together, stop // together, one, 0)
 
     wait_columns(have, near_x, near_g, near_fill)
+    for i in (1, 2):
+        sends[i].start()
     turn(near_x, near_xq, near_turned)
     for one in fills:
         one.wait()

time: 212 us -> 212 us (level)
  no operation moved by 1% of the time
where the time goes in v6:
time: 212 us; the launch traced here: 211 us
  Pallas kernels  203 us (96%)
  starting transfers between devices  3.83 us (2%)
  local copies, waits for them, and re-layouts  2.74 us (1%)
    pallas_call x1, Pallas kernels, gather_first(): pl.pallas_call(functools.partial(gather_kernel, zs), out_shape=jax.ShapeD...  87 us
    pallas_call x1, Pallas kernels, near_grads(): pl.pallas_call(functools.partial(grads_kernel, rows, first), out_shape=[s...  63.8 us
    pallas_call x1, Pallas kernels, far_grads(): pl.pallas_call(functools.partial(far_kernel, factor), out_shape=[shape, s...  29.2 us
    pallas_call x1, Pallas kernels, input_part(): pl.pallas_call(input_kernel, out_shape=jax.ShapeDtypeStruct((rows, featur...  22.5 us
  transfers between devices with their start and end apart: 1, of which 0 were waited for; matrix products, arithmetic and copies ran while one was open for 0% of the time, Pallas kernels for 44%

profile of v6, /device:TPU:0, one launch (start us, length us, event | category | flops | bytes accessed | tf_op | source)
XLA Modules:
  0.0 211.1 jit_solution(17899819238885024202)
XLA Ops:
  0.6 1.4 copy.9.ui
  2.0 1.4 copy.10.di
  3.4 87.0 %gather_first.1 = bf16[2,10,2,24,8192]{4,3,2,1,0:T(8,128)(2,1)} custom-call(bf16[24,8192]{1,0:T(8,128)(2,1)} %in_ref.1, bf16[24,8192]{1,0:T(8,128)(2,1)} %go_ref.1), custom_call_target="tpu_custom_call" | custom-call | tf_op jit(solution)/shard_map/gather_first/pallas_call | solution.py:179
  90.4 22.5 %input_part.1 = bf16[192,8192]{1,0:T(8,128)(2,1)} custom-call(s32[28,8]{1,0:T(8,128)} %copy.9.ui, s32[28,8]{1,0:T(8,128)} %copy.10.di, s32[1]{0:T(128)} %bitcast.pos, bf16[2,480,8192]{2,1,0:T(8,128)(2,1)} %bitcast.3, bf16[2,480,8192]{2,1,0:T(8,128)(2,1)} %bitcast.4, bf16[28,8,128,128]{3,2,1,0:T(8,128)(2,1)} %up_ref.3, bf16[28,8,128,128]{3,2,1,0:T(8,128)(2,1)} %down_ref.3), custom_call_target="tpu_custom_call" | custom-call | flops 4227858432 | bytes 24117248 | tf_op jit(solution)/shard_map/input_part/pallas_call | solution.py:257
  112.9 3.8 %all-to-all-start = ((bf16[8,24,8192]{2,1,0:T(8,128)(2,1)}), bf16[8,24,8192]{2,1,0:T(8,128)(2,1)S(1)}, u32[]{:S(2)}, u32[]{:S(2)}) async-start(bf16[8,24,8192]{2,1,0:T(8,128)(2,1)} %bitcast.6), calls=%async_computation | async-start | bytes 6291456 | tf_op jit(solution)/shard_map/all_to_all | solution.py:542
  116.7 63.8 %near_grads.1 = (f32[28,8,32,128]{3,2,1,0:T(8,128)}, f32[28,8,32,128]{3,2,1,0:T(8,128)}, bf16[2,288,8192]{2,1,0:T(8,128)(2,1)}) custom-call(s32[28,8]{1,0:T(8,128)} %copy.9.ui, s32[28,8]{1,0:T(8,128)} %copy.10.di, bf16[2,480,8192]{2,1,0:T(8,128)(2,1)} %bitcast.5, bf16[28,8,128,128]{3,2,1,0:T(8,128)(2,1)} %up_ref.3, bf16[28,8,128,128]{3,2,1,0:T(8,128)(2,1)} %down_ref.3), custom_call_target="tpu_custom_call" | custom-call | flops 10569646080 | bytes 45613056 | tf_op jit(solution)/shard_map/near_grads/pallas_call | solution.py:426
  180.6 29.2 %far_grads.1 = (bf16[28,8,32,128]{3,2,1,0:T(8,128)(2,1)}, bf16[28,8,32,128]{3,2,1,0:T(8,128)(2,1)}) custom-call(s32[28,8]{1,0:T(8,128)} %copy.9.ui, s32[28,8]{1,0:T(8,128)} %copy.10.di, s32[1]{0:T(128)} %bitcast.pos, bf16[2,288,8192]{2,1,0:T(8,128)(2,1)} %get-tuple-element.8.x_ref.g_ref, bf16[2,288,8192]{2,1,0:T(8,128)(2,1)} %get-tuple-element.8.x_ref.g_ref, ...), custom_call_target="tpu_custom_call" | custom-call | flops 6341787648 | bytes 31457280 | tf_op jit(solution)/shard_map/far_grads/pallas_call | solution.py:500
  209.8 0.0 all-to-all-done
  209.8 1.3 reduce_sum.12
Async XLA Ops:
  112.9 96.9 %all-to-all-start = ((bf16[8,24,8192]{2,1,0:T(8,128)(2,1)}), bf16[8,24,8192]{2,1,0:T(8,128)(2,1)S(1)}, u32[]{:S(2)}, u32[]{:S(2)}) async-start(bf16[8,24,8192]{2,1,0:T(8,128)(2,1)} %bitcast.6), calls=%async_computation | async-start | bytes 6291456 | tf_op jit(solution)/shard_map/all_to_all | solution.py:542
